TPU v7x, 256 devices: a whole 4x4x8 slice. The times are simulated.
256 devices in a mesh: alt: 64 (over y, z, core), raan: 4 (over x).
Axes of the slice: x: 4, y: 4, z: 8, core: 2. Of those that a mesh axis runs over, the one named last changes fastest.
Arguments:
- source: float32 [256, 64, 1024], P('alt', None, 'raan'), may hold values from -6 to 6
- k_alt: float32 [256, 64, 1024], P('alt', None, 'raan'), may hold values from 20 to 400
- k_inc: float32 [256, 64, 1024], P('alt', None, 'raan'), may hold values from 20 to 400
- k_raan: float32 [256, 64, 1024], P('alt', None, 'raan'), may hold values from 20 to 400
Outputs:
- density: float32 [256, 64, 1024], P('alt', None, 'raan')
- scaled_residual: float32 [256, 64, 1024], P('alt', None, 'raan')
All inputs are finite; a program needn't handle non-finite values.
Results may differ from a plain program's by a relative error of at most 0.00018.
Values sent between devices are 32-bit elements; how exact they have to be, the bound alone decides.
A program may use at most 128 MiB of HBM per device.

v0:
```python
import jax
import jax.numpy as jnp
from jax import lax
from jax.sharding import PartitionSpec as P

SWEEPS = 2
COARSE_SWEEPS = 4


OMEGA = 0.75


def with_halo(shard, sides, width, wrap):
    for axis, dim in sides:
        count, length = (lax.axis_size(axis), shard.shape[dim])
        up = [(i, (i + 1) % count) for i in range(count if wrap else count - 1)]
        down = [(j, i) for i, j in up]
        last = lax.slice_in_dim(shard, length - width, length, axis=dim)
        leading = lax.slice_in_dim(shard, 0, width, axis=dim)
        before = lax.ppermute(last, axis, up)
        after = lax.ppermute(leading, axis, down)
        shard = jnp.concatenate([before, shard, after], axis=dim)
    return shard


def shifted(block, axis, distance):
    devices = range(lax.axis_size(axis))
    route = [(i - distance, i) for i in devices if i - distance in devices]
    return lax.ppermute(block, axis, route)


def from_partner(block, axis, distance):
    count = lax.axis_size(axis)
    route = []
    for low in range(count):
        high = low | 1 << distance
        if high != low and high < count:
            route += [(low, high), (high, low)]
    return lax.ppermute(block, axis, route)


def coarsen(values):
    depth, width, length = values.shape
    return values.reshape(depth // 2, 2, width // 2, 2, length // 2, 2).mean(axis=(1, 3, 5))


def refine(values):
    return jnp.repeat(jnp.repeat(jnp.repeat(values, 2, 0), 2, 1), 2, 2)


def alt_ext(values):
    return with_halo(values, (("alt", 0),), 1, False)


def raan_ext(values):
    return with_halo(values, (("raan", 2),), 1, True)


def plain_alt(values):
    padded = alt_ext(values)
    return (padded[:-2], padded[2:])


def fold_alt(values):
    below = shifted(values[-1:], "alt", 2)
    above = shifted(values[:1], "alt", -2)
    v_down = jnp.concatenate([below, values[:-1]], 0)
    v_up = jnp.concatenate([values[1:], above], 0)
    return (v_down, v_up)


def field_near(field):
    v_down, v_up = plain_alt(field)
    wrapped = raan_ext(field)
    return (v_down, v_up, wrapped[:, :, :-2], wrapped[:, :, 2:])


def fold_near(field):
    v_down, v_up = fold_alt(field)
    wrapped = raan_ext(field)
    return (v_down, v_up, wrapped[:, :, :-2], wrapped[:, :, 2:])


def make_weights(coef_alt, coef_inc, coef_raan, factor, alt_pair):
    alt_down, alt_up = alt_pair(coef_alt)
    w_alt_lo = factor * 0.5 * (coef_alt + alt_down)
    w_alt_hi = factor * 0.5 * (coef_alt + alt_up)
    inner_faces = factor * 0.5 * (coef_inc[:, :-1] + coef_inc[:, 1:])
    zero_inc = jnp.zeros_like(coef_inc[:, :1])
    w_inc_lo = jnp.concatenate([zero_inc, inner_faces], 1)
    w_inc_hi = jnp.concatenate([inner_faces, zero_inc], 1)
    wrapped = raan_ext(coef_raan)
    w_raan_lo = factor * 0.5 * (coef_raan + wrapped[:, :, :-2])
    w_raan_hi = factor * 0.5 * (coef_raan + wrapped[:, :, 2:])
    diagonal = 1.0 + (w_alt_lo + w_alt_hi + w_inc_lo + w_inc_hi + w_raan_lo + w_raan_hi)
    return (w_alt_lo, w_alt_hi, w_inc_lo, w_inc_hi, w_raan_lo, w_raan_hi, diagonal)


def apply_op(weights, field, near):
    w_alt_lo, w_alt_hi, w_inc_lo, w_inc_hi, w_raan_lo, w_raan_hi, diagonal = weights
    v_down, v_up, v_left, v_right = near(field)
    zero_inc = jnp.zeros_like(field[:, :1])
    v_prev = jnp.concatenate([zero_inc, field[:, :-1]], 1)
    v_next = jnp.concatenate([field[:, 1:], zero_inc], 1)
    beside = (
        w_alt_lo * v_down
        + w_alt_hi * v_up
        + w_inc_lo * v_prev
        + w_inc_hi * v_next
        + w_raan_lo * v_left
        + w_raan_hi * v_right
    )
    return diagonal * field - beside


def smooth(field, target, weights, near, repeats):
    for _ in range(repeats):
        field = field + OMEGA * (target - apply_op(weights, field, near)) / weights[6]
    return field


def coarse_solve(target, weights, near):
    field = OMEGA * target / weights[6]
    return smooth(field, target, weights, near, COARSE_SWEEPS - 1)


def shards(source, k_alt, k_inc, k_raan):
    weights_one = make_weights(k_alt, k_inc, k_raan, 1.0, plain_alt)
    coef_two = (coarsen(k_alt), coarsen(k_inc), coarsen(k_raan))
    weights_two = make_weights(coef_two[0], coef_two[1], coef_two[2], 0.25, plain_alt)
    coef_three = (coarsen(coef_two[0]), coarsen(coef_two[1]), coarsen(coef_two[2]))
    density = smooth(source, source, weights_one, field_near, SWEEPS)
    rhs_two = coarsen(source - apply_op(weights_one, density, field_near))
    correction = OMEGA * rhs_two / weights_two[6]
    correction = smooth(correction, rhs_two, weights_two, field_near, SWEEPS - 1)
    rhs_three = coarsen(rhs_two - apply_op(weights_two, correction, field_near))
    height = rhs_three.shape[0]
    parity = lax.axis_index("alt") % 2
    own_part = jnp.stack((rhs_three, coef_three[0], coef_three[1], coef_three[2]))
    theirs = from_partner(own_part, "alt", 0)
    low_half = jnp.where(parity == 0, own_part, theirs)
    high_half = jnp.where(parity == 0, theirs, own_part)
    pair_block = jnp.concatenate([low_half, high_half], axis=1)
    weights_three = make_weights(pair_block[1], pair_block[2], pair_block[3], 0.0625, fold_alt)
    pair_result = coarse_solve(pair_block[0], weights_three, fold_near)
    coarse_part = lax.dynamic_slice_in_dim(pair_result, parity * height, height, 0)
    correction = correction + refine(coarse_part)
    correction = smooth(correction, rhs_two, weights_two, field_near, SWEEPS)
    density = density + refine(correction)
    density = smooth(density, source, weights_one, field_near, SWEEPS)
    scaled_residual = (source - apply_op(weights_one, density, field_near)) / weights_one[6]
    return (density, scaled_residual)


def solution(mesh):
    in_specs = (
        P("alt", None, "raan"),
        P("alt", None, "raan"),
        P("alt", None, "raan"),
        P("alt", None, "raan"),
    )
    out_specs = (P("alt", None, "raan"), P("alt", None, "raan"))
    return jax.shard_map(shards, mesh=mesh, in_specs=in_specs, out_specs=out_specs, check_vma=False)
```

profile of v0, /device:TPU:24, one launch (start us, length us, event | category | flops | bytes accessed | tf_op | source)
XLA Modules:
  0.0 337.4 jit_solution(17884741008604837807)
XLA Ops:
  4.5 7.4 %collective-permute-start.1 = (f32[1,64,256]{1,2,0:T(8,128)}, f32[1,64,256]{1,2,0:T(8,128)S(1)}, u32[]{:S(2)}, u32[]{:S(2)}) collective-permute-start(f32[1,64,256]{1,2,0:T(8,128)} %get-tuple-element.46), channel_id=1, source_target_pairs={{4,0},{8,4},{12,8},{16,12},{20,16},{24,20},{28,24},{32,28},{36,32}... | collective-permute-start | bytes 196616 | tf_op jit(solution)/shard_map/ppermute | solution.py:21
  19.8 18.9 %reshape.97 = f32[2,2,32,2,128,2]{5,4,3,2,1,0:T(8,128)} reshape(f32[4,64,256]{2,1,0:T(8,128)} %param.5) | data formatting | bytes 524288 | tf_op jit(solution)/shard_map/reshape | solution.py:44
  38.7 18.1 %reshape.98 = f32[2,2,32,2,128,2]{5,4,3,2,1,0:T(8,128)} reshape(f32[4,64,256]{2,1,0:T(8,128)S(1)} %copy-done) | data formatting | bytes 524288 | tf_op jit(solution)/shard_map/reshape | solution.py:44
  56.8 18.1 %reshape.99 = f32[2,2,32,2,128,2]{5,4,3,2,1,0:T(8,128)} reshape(f32[4,64,256]{2,1,0:T(8,128)S(1)} %copy-done.1) | data formatting | bytes 524288 | tf_op jit(solution)/shard_map/reshape | solution.py:44
  76.1 7.0 %reduce_sum.82 = f32[2,32,128]{2,1,0:T(8,128)S(1)} reduce(f32[2,2,32,2,128,2]{5,4,3,2,1,0:T(8,128)} %reshape.97, f32[]{:T(128)} %constant.19.clone.1), dimensions={1,3,5}, to_apply=%region_1.0 | reduce | flops 57344 | bytes 294916 | tf_op jit(solution)/shard_map/reduce_sum | solution.py:44
  83.7 7.0 %reduce_sum.83 = f32[2,32,128]{2,1,0:T(8,128)S(1)} reduce(f32[2,2,32,2,128,2]{5,4,3,2,1,0:T(8,128)} %reshape.98, f32[]{:T(128)} %constant.19.clone.1), dimensions={1,3,5}, to_apply=%region_2.0 | reduce | flops 57344 | bytes 294916 | tf_op jit(solution)/shard_map/reduce_sum | solution.py:44
  90.7 7.0 %reduce_sum.87 = f32[2,32,128]{2,1,0:T(8,128)S(1)} reduce(f32[2,2,32,2,128,2]{5,4,3,2,1,0:T(8,128)} %reshape.99, f32[]{:T(128)} %constant.19.clone.1), dimensions={1,3,5}, to_apply=%region_3.0 | reduce | flops 57344 | bytes 294916 | tf_op jit(solution)/shard_map/reduce_sum | solution.py:44
  102.1 2.1 fusion.227
  104.8 2.0 reduce_sum.108
  110.2 5.8 %collective-permute-start.5 = (f32[1,64,256]{1,2,0:T(8,128)}, f32[1,64,256]{1,2,0:T(8,128)S(1)}, u32[]{:S(2)}, u32[]{:S(2)}) collective-permute-start(f32[1,64,256]{1,2,0:T(8,128)} %get-tuple-element.53), channel_id=1, source_target_pairs={{4,0},{8,4},{12,8},{16,12},{20,16},{24,20},{28,24},{32,28},{36,32}... | collective-permute-start | bytes 196616 | tf_op jit(solution)/shard_map/ppermute | solution.py:21
  116.5 3.0 collective-permute-start.7
  120.8 2.1 collective-permute-start.16
  123.0 2.0 fusion.71
  125.0 1.9 collective-permute-start.8
  127.0 5.8 %collective-permute-start.9 = (f32[1,64,256]{1,2,0:T(8,128)S(1)}, f32[1,64,256]{1,2,0:T(8,128)S(1)}, u32[]{:S(2)}, u32[]{:S(2)}) collective-permute-start(f32[1,64,256]{1,2,0:T(8,128)S(1)} %get-tuple-element.43), channel_id=1, source_target_pairs={{4,0},{8,4},{12,8},{16,12},{20,16},{24,20},{28,24},{32,28},{36,32}... | collective-permute-start | bytes 196616 | tf_op jit(solution)/shard_map/ppermute | solution.py:21
  133.6 2.8 collective-permute-start.11
  138.8 1.9 collective-permute-start.12
  140.8 5.8 %collective-permute-start.13 = (f32[1,64,256]{1,2,0:T(8,128)S(1)}, f32[1,64,256]{1,2,0:T(8,128)S(1)}, u32[]{:S(2)}, u32[]{:S(2)}) collective-permute-start(f32[1,64,256]{1,2,0:T(8,128)S(1)} %get-tuple-element.37), channel_id=1, source_target_pairs={{4,0},{8,4},{12,8},{16,12},{20,16},{24,20},{28,24},{32,28},{36,32}... | collective-permute-start | bytes 196616 | tf_op jit(solution)/shard_map/ppermute | solution.py:21
  148.0 2.0 collective-permute-start.15
  153.6 3.1 collective-permute-start.19
  158.5 18.9 %reshape.96 = f32[2,2,32,2,128,2]{5,4,3,2,1,0:T(8,128)} reshape(f32[4,64,256]{2,1,0:T(8,128)} %copy.70) | data formatting | bytes 524288 | tf_op jit(solution)/shard_map/reshape | solution.py:44
  177.3 7.0 %reduce_sum.81 = f32[2,32,128]{2,1,0:T(8,128)S(1)} reduce(f32[2,2,32,2,128,2]{5,4,3,2,1,0:T(8,128)} %reshape.96, f32[]{:T(128)} %constant.19.clone.1), dimensions={1,3,5}, to_apply=%region_0.0 | reduce | flops 57344 | bytes 294916 | tf_op jit(solution)/shard_map/reduce_sum | solution.py:44
  185.4 3.6 %collective-permute-start.23 = (f32[2,32,1]{2,1,0:T(8,128)S(1)}, f32[2,32,1]{2,1,0:T(8,128)S(1)}, u32[]{:S(2)}, u32[]{:S(2)}) collective-permute-start(f32[2,32,1]{2,1,0:T(8,128)S(1)} %get-tuple-element.91), channel_id=1, source_target_pairs={{1,0},{2,1},{3,2},{0,3},{5,4},{6,5},{7,6},{4,7},{9,8},{10,9},{11,1... | collective-permute-start | bytes 776 | tf_op jit(solution)/shard_map/ppermute | solution.py:21
  190.9 5.8 %collective-permute-start.21 = (f32[1,32,128]{2,1,0:T(8,128)S(1)}, f32[1,32,128]{2,1,0:T(8,128)S(1)}, u32[]{:S(2)}, u32[]{:S(2)}) collective-permute-start(f32[1,32,128]{2,1,0:T(8,128)S(1)} %get-tuple-element.89), channel_id=1, source_target_pairs={{4,0},{8,4},{12,8},{16,12},{20,16},{24,20},{28,24},{32,28},{36,32}... | collective-permute-start | bytes 49160 | tf_op jit(solution)/shard_map/ppermute | solution.py:21
  198.3 3.2 collective-permute-start.27
  203.5 5.8 %collective-permute-start.25 = (f32[1,32,128]{2,1,0:T(8,128)S(1)}, f32[1,32,128]{2,1,0:T(8,128)S(1)}, u32[]{:S(2)}, u32[]{:S(2)}) collective-permute-start(f32[1,32,128]{2,1,0:T(8,128)S(1)} %get-tuple-element.77), channel_id=1, source_target_pairs={{4,0},{8,4},{12,8},{16,12},{20,16},{24,20},{28,24},{32,28},{36,32}... | collective-permute-start | bytes 49160 | tf_op jit(solution)/shard_map/ppermute | solution.py:21
  210.7 2.0 reduce_sum.105
  215.7 3.2 collective-permute-start.32
  220.8 6.0 %collective-permute-start.30 = (f32[1,16,64]{2,1,0:T(8,128)S(1)}, f32[1,16,64]{2,1,0:T(8,128)S(1)}, u32[]{:S(2)}, u32[]{:S(2)}) collective-permute-start(f32[1,16,64]{2,1,0:T(8,128)S(1)} %slice_bitcast_fusion), channel_id=1, source_target_pairs={{8,0},{12,4},{16,8},{20,12},{24,16},{28,20},{32,24},{36,28},{40,32... | collective-permute-start | bytes 12296 | tf_op jit(solution)/shard_map/ppermute | solution.py:29
  228.4 3.2 collective-permute-start.36
  233.5 6.3 %collective-permute-start.34 = (f32[1,16,64]{2,1,0:T(8,128)S(1)}, f32[1,16,64]{2,1,0:T(8,128)S(1)}, u32[]{:S(2)}, u32[]{:S(2)}) collective-permute-start(f32[1,16,64]{2,1,0:T(8,128)S(1)} %get-tuple-element.113), channel_id=1, source_target_pairs={{8,0},{12,4},{16,8},{20,12},{24,16},{28,20},{32,24},{36,28},{40,32... | collective-permute-start | bytes 12296 | tf_op jit(solution)/shard_map/ppermute | solution.py:29
  241.4 3.2 collective-permute-start.40
  246.5 6.3 %collective-permute-start.38 = (f32[1,16,64]{2,1,0:T(8,128)S(1)}, f32[1,16,64]{2,1,0:T(8,128)S(1)}, u32[]{:S(2)}, u32[]{:S(2)}) collective-permute-start(f32[1,16,64]{2,1,0:T(8,128)S(1)} %get-tuple-element.107), channel_id=1, source_target_pairs={{8,0},{12,4},{16,8},{20,12},{24,16},{28,20},{32,24},{36,28},{40,32... | collective-permute-start | bytes 12296 | tf_op jit(solution)/shard_map/ppermute | solution.py:29
  254.4 3.2 collective-permute-start.44
  259.5 6.3 %collective-permute-start.42 = (f32[1,16,64]{2,1,0:T(8,128)S(1)}, f32[1,16,64]{2,1,0:T(8,128)S(1)}, u32[]{:S(2)}, u32[]{:S(2)}) collective-permute-start(f32[1,16,64]{2,1,0:T(8,128)S(1)} %get-tuple-element.101), channel_id=1, source_target_pairs={{8,0},{12,4},{16,8},{20,12},{24,16},{28,20},{32,24},{36,28},{40,32... | collective-permute-start | bytes 12296 | tf_op jit(solution)/shard_map/ppermute | solution.py:29
  267.7 3.2 collective-permute-start.48
  272.8 5.8 %collective-permute-start.46 = (f32[1,32,128]{2,1,0:T(8,128)S(1)}, f32[1,32,128]{2,1,0:T(8,128)S(1)}, u32[]{:S(2)}, u32[]{:S(2)}) collective-permute-start(f32[1,32,128]{2,1,0:T(8,128)S(1)} %get-tuple-element.71), channel_id=1, source_target_pairs={{4,0},{8,4},{12,8},{16,12},{20,16},{24,20},{28,24},{32,28},{36,32}... | collective-permute-start | bytes 49160 | tf_op jit(solution)/shard_map/ppermute | solution.py:21
  280.4 3.2 collective-permute-start.52
  285.5 5.8 %collective-permute-start.50 = (f32[1,32,128]{2,1,0:T(8,128)S(1)}, f32[1,32,128]{2,1,0:T(8,128)S(1)}, u32[]{:S(2)}, u32[]{:S(2)}) collective-permute-start(f32[1,32,128]{2,1,0:T(8,128)S(1)} %get-tuple-element.65), channel_id=1, source_target_pairs={{4,0},{8,4},{12,8},{16,12},{20,16},{24,20},{28,24},{32,28},{36,32}... | collective-permute-start | bytes 49160 | tf_op jit(solution)/shard_map/ppermute | solution.py:21
  293.3 1.9 collective-permute-start.53
  295.2 5.8 %collective-permute-start.54 = (f32[1,64,256]{1,2,0:T(8,128)S(1)}, f32[1,64,256]{1,2,0:T(8,128)S(1)}, u32[]{:S(2)}, u32[]{:S(2)}) collective-permute-start(f32[1,64,256]{1,2,0:T(8,128)S(1)} %get-tuple-element.31), channel_id=1, source_target_pairs={{4,0},{8,4},{12,8},{16,12},{20,16},{24,20},{28,24},{32,28},{36,32}... | collective-permute-start | bytes 196616 | tf_op jit(solution)/shard_map/ppermute | solution.py:21
  301.1 3.2 collective-permute-start.56
  308.8 5.8 %collective-permute-start.58 = (f32[1,64,256]{1,2,0:T(8,128)S(1)}, f32[1,64,256]{1,2,0:T(8,128)S(1)}, u32[]{:S(2)}, u32[]{:S(2)}) collective-permute-start(f32[1,64,256]{1,2,0:T(8,128)S(1)} %get-tuple-element.25), channel_id=1, source_target_pairs={{4,0},{8,4},{12,8},{16,12},{20,16},{24,20},{28,24},{32,28},{36,32}... | collective-permute-start | bytes 196616 | tf_op jit(solution)/shard_map/ppermute | solution.py:21
  314.6 3.3 collective-permute-start.60
  320.4 1.9 collective-permute-start.61
  322.3 5.8 %collective-permute-start.62 = (f32[1,64,256]{1,2,0:T(8,128)S(1)}, f32[1,64,256]{1,2,0:T(8,128)S(1)}, u32[]{:S(2)}, u32[]{:S(2)}) collective-permute-start(f32[1,64,256]{1,2,0:T(8,128)S(1)} %get-tuple-element.19), channel_id=1, source_target_pairs={{4,0},{8,4},{12,8},{16,12},{20,16},{24,20},{28,24},{32,28},{36,32}... | collective-permute-start | bytes 196616 | tf_op jit(solution)/shard_map/ppermute | solution.py:21
  329.6 2.0 collective-permute-start.64
  334.3 2.1 fusion.4
  (202 shorter events, 78.4 us)
Async XLA Ops:
  2.6 120.4 %collective-permute-start = (f32[1,64,256]{1,2,0:T(8,128)}, f32[1,64,256]{1,2,0:T(8,128)S(1)}, u32[]{:S(2)}, u32[]{:S(2)}) collective-permute-start(f32[1,64,256]{1,2,0:T(8,128)} %get-tuple-element.47), channel_id=1, source_target_pairs={{0,4},{4,8},{8,12},{12,16},{16,20},{20,24},{24,28},{28,32},{32,36}... | collective-permute-start | bytes 196616 | tf_op jit(solution)/shard_map/ppermute | solution.py:20
  4.5 118.5 %collective-permute-start.1 = (f32[1,64,256]{1,2,0:T(8,128)}, f32[1,64,256]{1,2,0:T(8,128)S(1)}, u32[]{:S(2)}, u32[]{:S(2)}) collective-permute-start(f32[1,64,256]{1,2,0:T(8,128)} %get-tuple-element.46), channel_id=1, source_target_pairs={{4,0},{8,4},{12,8},{16,12},{20,16},{24,20},{28,24},{32,28},{36,32}... | collective-permute-start | bytes 196616 | tf_op jit(solution)/shard_map/ppermute | solution.py:21
  13.6 94.6 %collective-permute-start.2 = (f32[4,64,1]{1,2,0:T(1,128)}, f32[4,64,1]{1,2,0:T(1,128)S(1)}, u32[]{:S(2)}, u32[]{:S(2)}) collective-permute-start(f32[4,64,1]{1,2,0:T(1,128)} %get-tuple-element.49), channel_id=1, source_target_pairs={{0,1},{1,2},{2,3},{3,0},{4,5},{5,6},{6,7},{7,4},{8,9},{9,10},{10,1... | collective-permute-start | bytes 3080 | tf_op jit(solution)/shard_map/ppermute | solution.py:20
  15.1 95.0 %collective-permute-start.3 = (f32[4,64,1]{1,2,0:T(1,128)S(1)}, f32[4,64,1]{1,2,0:T(1,128)S(1)}, u32[]{:S(2)}, u32[]{:S(2)}) collective-permute-start(f32[4,64,1]{1,2,0:T(1,128)S(1)} %get-tuple-element.48), channel_id=1, source_target_pairs={{1,0},{2,1},{3,2},{0,3},{5,4},{6,5},{7,6},{4,7},{9,8},{10,9},{11,1... | collective-permute-start | bytes 3080 | tf_op jit(solution)/shard_map/ppermute | solution.py:21
  18.6 97.3 %collective-permute-start.6 = (f32[4,64,1]{1,2,0:T(1,128)}, f32[4,64,1]{1,2,0:T(1,128)S(1)}, u32[]{:S(2)}, u32[]{:S(2)}) collective-permute-start(f32[4,64,1]{1,2,0:T(1,128)} %get-tuple-element.54), channel_id=1, source_target_pairs={{0,1},{1,2},{2,3},{3,0},{4,5},{5,6},{6,7},{7,4},{8,9},{9,10},{10,1... | collective-permute-start | bytes 3080 | tf_op jit(solution)/shard_map/ppermute | solution.py:20
  108.2 14.8 %collective-permute-start.4 = (f32[1,64,256]{1,2,0:T(8,128)}, f32[1,64,256]{1,2,0:T(8,128)S(1)}, u32[]{:S(2)}, u32[]{:S(2)}) collective-permute-start(f32[1,64,256]{1,2,0:T(8,128)} %get-tuple-element.52), channel_id=1, source_target_pairs={{0,4},{4,8},{8,12},{12,16},{16,20},{20,24},{24,28},{28,32},{32,36}... | collective-permute-start | bytes 196616 | tf_op jit(solution)/shard_map/ppermute | solution.py:20
  110.2 12.8 %collective-permute-start.5 = (f32[1,64,256]{1,2,0:T(8,128)}, f32[1,64,256]{1,2,0:T(8,128)S(1)}, u32[]{:S(2)}, u32[]{:S(2)}) collective-permute-start(f32[1,64,256]{1,2,0:T(8,128)} %get-tuple-element.53), channel_id=1, source_target_pairs={{4,0},{8,4},{12,8},{16,12},{20,16},{24,20},{28,24},{32,28},{36,32}... | collective-permute-start | bytes 196616 | tf_op jit(solution)/shard_map/ppermute | solution.py:21
  120.8 63.5 %collective-permute-start.16 = (f32[1,32,128]{2,1,0:T(8,128)}, f32[1,32,128]{2,1,0:T(8,128)S(1)}, u32[]{:S(2)}, u32[]{:S(2)}) collective-permute-start(f32[1,32,128]{2,1,0:T(8,128)} %get-tuple-element.95), channel_id=1, source_target_pairs={{0,4},{4,8},{8,12},{12,16},{16,20},{20,24},{24,28},{28,32},{32,36}... | collective-permute-start | bytes 49160 | tf_op jit(solution)/shard_map/ppermute | solution.py:20
  125.0 12.8 %collective-permute-start.8 = (f32[1,64,256]{1,2,0:T(8,128)S(1)}, f32[1,64,256]{1,2,0:T(8,128)S(1)}, u32[]{:S(2)}, u32[]{:S(2)}) collective-permute-start(f32[1,64,256]{1,2,0:T(8,128)S(1)} %get-tuple-element.42), channel_id=1, source_target_pairs={{0,4},{4,8},{8,12},{12,16},{16,20},{20,24},{24,28},{28,32},{32,36}... | collective-permute-start | bytes 196616 | tf_op jit(solution)/shard_map/ppermute | solution.py:20
  127.0 10.9 %collective-permute-start.9 = (f32[1,64,256]{1,2,0:T(8,128)S(1)}, f32[1,64,256]{1,2,0:T(8,128)S(1)}, u32[]{:S(2)}, u32[]{:S(2)}) collective-permute-start(f32[1,64,256]{1,2,0:T(8,128)S(1)} %get-tuple-element.43), channel_id=1, source_target_pairs={{4,0},{8,4},{12,8},{16,12},{20,16},{24,20},{28,24},{32,28},{36,32}... | collective-permute-start | bytes 196616 | tf_op jit(solution)/shard_map/ppermute | solution.py:21
  138.8 14.8 %collective-permute-start.12 = (f32[1,64,256]{1,2,0:T(8,128)S(1)}, f32[1,64,256]{1,2,0:T(8,128)S(1)}, u32[]{:S(2)}, u32[]{:S(2)}) collective-permute-start(f32[1,64,256]{1,2,0:T(8,128)S(1)} %get-tuple-element.36), channel_id=1, source_target_pairs={{0,4},{4,8},{8,12},{12,16},{16,20},{20,24},{24,28},{28,32},{32,36}... | collective-permute-start | bytes 196616 | tf_op jit(solution)/shard_map/ppermute | solution.py:20
  140.8 16.0 %collective-permute-start.13 = (f32[1,64,256]{1,2,0:T(8,128)S(1)}, f32[1,64,256]{1,2,0:T(8,128)S(1)}, u32[]{:S(2)}, u32[]{:S(2)}) collective-permute-start(f32[1,64,256]{1,2,0:T(8,128)S(1)} %get-tuple-element.37), channel_id=1, source_target_pairs={{4,0},{8,4},{12,8},{16,12},{20,16},{24,20},{28,24},{32,28},{36,32}... | collective-permute-start | bytes 196616 | tf_op jit(solution)/shard_map/ppermute | solution.py:21
  151.5 32.9 %collective-permute-start.17 = (f32[1,32,128]{2,1,0:T(8,128)}, f32[1,32,128]{2,1,0:T(8,128)S(1)}, u32[]{:S(2)}, u32[]{:S(2)}) collective-permute-start(f32[1,32,128]{2,1,0:T(8,128)} %get-tuple-element.94), channel_id=1, source_target_pairs={{4,0},{8,4},{12,8},{16,12},{20,16},{24,20},{28,24},{32,28},{36,32}... | collective-permute-start | bytes 49160 | tf_op jit(solution)/shard_map/ppermute | solution.py:21
  153.4 30.9 %collective-permute-start.18 = (f32[2,32,1]{2,1,0:T(8,128)}, f32[2,32,1]{2,1,0:T(8,128)}, u32[]{:S(2)}, u32[]{:S(2)}) collective-permute-start(f32[2,32,1]{2,1,0:T(8,128)} %get-tuple-element.93), channel_id=1, source_target_pairs={{0,1},{1,2},{2,3},{3,0},{4,5},{5,6},{6,7},{7,4},{8,9},{9,10},{10,1... | collective-permute-start | bytes 776 | tf_op jit(solution)/shard_map/ppermute | solution.py:20
  153.6 30.7 %collective-permute-start.19 = (f32[2,32,1]{2,1,0:T(8,128)}, f32[2,32,1]{2,1,0:T(8,128)}, u32[]{:S(2)}, u32[]{:S(2)}) collective-permute-start(f32[2,32,1]{2,1,0:T(8,128)} %get-tuple-element.92), channel_id=1, source_target_pairs={{1,0},{2,1},{3,2},{0,3},{5,4},{6,5},{7,6},{4,7},{9,8},{10,9},{11,1... | collective-permute-start | bytes 776 | tf_op jit(solution)/shard_map/ppermute | solution.py:21
  185.3 11.4 %collective-permute-start.22 = (f32[2,32,1]{2,1,0:T(8,128)S(1)}, f32[2,32,1]{2,1,0:T(8,128)S(1)}, u32[]{:S(2)}, u32[]{:S(2)}) collective-permute-start(f32[2,32,1]{2,1,0:T(8,128)S(1)} %get-tuple-element.90), channel_id=1, source_target_pairs={{0,1},{1,2},{2,3},{3,0},{4,5},{5,6},{6,7},{7,4},{8,9},{9,10},{10,1... | collective-permute-start | bytes 776 | tf_op jit(solution)/shard_map/ppermute | solution.py:20
  185.4 11.3 %collective-permute-start.23 = (f32[2,32,1]{2,1,0:T(8,128)S(1)}, f32[2,32,1]{2,1,0:T(8,128)S(1)}, u32[]{:S(2)}, u32[]{:S(2)}) collective-permute-start(f32[2,32,1]{2,1,0:T(8,128)S(1)} %get-tuple-element.91), channel_id=1, source_target_pairs={{1,0},{2,1},{3,2},{0,3},{5,4},{6,5},{7,6},{4,7},{9,8},{10,9},{11,1... | collective-permute-start | bytes 776 | tf_op jit(solution)/shard_map/ppermute | solution.py:21
  189.0 7.7 %collective-permute-start.20 = (f32[1,32,128]{2,1,0:T(8,128)S(1)}, f32[1,32,128]{2,1,0:T(8,128)S(1)}, u32[]{:S(2)}, u32[]{:S(2)}) collective-permute-start(f32[1,32,128]{2,1,0:T(8,128)S(1)} %get-tuple-element.88), channel_id=1, source_target_pairs={{0,4},{4,8},{8,12},{12,16},{16,20},{20,24},{24,28},{28,32},{32,36}... | collective-permute-start | bytes 49160 | tf_op jit(solution)/shard_map/ppermute | solution.py:20
  198.3 11.0 %collective-permute-start.26 = (f32[2,32,1]{2,1,0:T(8,128)S(1)}, f32[2,32,1]{2,1,0:T(8,128)S(1)}, u32[]{:S(2)}, u32[]{:S(2)}) collective-permute-start(f32[2,32,1]{2,1,0:T(8,128)S(1)} %get-tuple-element.78), channel_id=1, source_target_pairs={{0,1},{1,2},{2,3},{3,0},{4,5},{5,6},{6,7},{7,4},{8,9},{9,10},{10,1... | collective-permute-start | bytes 776 | tf_op jit(solution)/shard_map/ppermute | solution.py:20
  198.3 10.9 %collective-permute-start.27 = (f32[2,32,1]{2,1,0:T(8,128)S(1)}, f32[2,32,1]{2,1,0:T(8,128)S(1)}, u32[]{:S(2)}, u32[]{:S(2)}) collective-permute-start(f32[2,32,1]{2,1,0:T(8,128)S(1)} %get-tuple-element.79), channel_id=1, source_target_pairs={{1,0},{2,1},{3,2},{0,3},{5,4},{6,5},{7,6},{4,7},{9,8},{10,9},{11,1... | collective-permute-start | bytes 776 | tf_op jit(solution)/shard_map/ppermute | solution.py:21
  201.5 7.7 %collective-permute-start.24 = (f32[1,32,128]{2,1,0:T(8,128)S(1)}, f32[1,32,128]{2,1,0:T(8,128)S(1)}, u32[]{:S(2)}, u32[]{:S(2)}) collective-permute-start(f32[1,32,128]{2,1,0:T(8,128)S(1)} %get-tuple-element.76), channel_id=1, source_target_pairs={{0,4},{4,8},{8,12},{12,16},{16,20},{20,24},{24,28},{28,32},{32,36}... | collective-permute-start | bytes 49160 | tf_op jit(solution)/shard_map/ppermute | solution.py:20
  215.6 11.2 %collective-permute-start.31 = (f32[2,16,1]{2,1,0:T(8,128)S(1)}, f32[2,16,1]{2,1,0:T(8,128)S(1)}, u32[]{:S(2)}, u32[]{:S(2)}) collective-permute-start(f32[2,16,1]{2,1,0:T(8,128)S(1)} %get-tuple-element.117), channel_id=1, source_target_pairs={{0,1},{1,2},{2,3},{3,0},{4,5},{5,6},{6,7},{7,4},{8,9},{9,10},{10,1... | collective-permute-start | bytes 392 | tf_op jit(solution)/shard_map/ppermute | solution.py:20
  215.7 11.2 %collective-permute-start.32 = (f32[2,16,1]{2,1,0:T(8,128)S(1)}, f32[2,16,1]{2,1,0:T(8,128)S(1)}, u32[]{:S(2)}, u32[]{:S(2)}) collective-permute-start(f32[2,16,1]{2,1,0:T(8,128)S(1)} %get-tuple-element.116), channel_id=1, source_target_pairs={{1,0},{2,1},{3,2},{0,3},{5,4},{6,5},{7,6},{4,7},{9,8},{10,9},{11,1... | collective-permute-start | bytes 392 | tf_op jit(solution)/shard_map/ppermute | solution.py:21
  218.9 8.0 %collective-permute-start.29 = (f32[1,16,64]{2,1,0:T(8,128)S(1)}, f32[1,16,64]{2,1,0:T(8,128)S(1)}, u32[]{:S(2)}, u32[]{:S(2)}) collective-permute-start(f32[1,16,64]{2,1,0:T(8,128)S(1)} %slice_bitcast_fusion.1), channel_id=1, source_target_pairs={{0,8},{4,12},{8,16},{12,20},{16,24},{20,28},{24,32},{28,36},{32,40... | collective-permute-start | bytes 12296 | tf_op jit(solution)/shard_map/ppermute | solution.py:29
  228.4 11.5 %collective-permute-start.35 = (f32[2,16,1]{2,1,0:T(8,128)S(1)}, f32[2,16,1]{2,1,0:T(8,128)S(1)}, u32[]{:S(2)}, u32[]{:S(2)}) collective-permute-start(f32[2,16,1]{2,1,0:T(8,128)S(1)} %get-tuple-element.114), channel_id=1, source_target_pairs={{0,1},{1,2},{2,3},{3,0},{4,5},{5,6},{6,7},{7,4},{8,9},{9,10},{10,1... | collective-permute-start | bytes 392 | tf_op jit(solution)/shard_map/ppermute | solution.py:20
  228.4 11.5 %collective-permute-start.36 = (f32[2,16,1]{2,1,0:T(8,128)S(1)}, f32[2,16,1]{2,1,0:T(8,128)S(1)}, u32[]{:S(2)}, u32[]{:S(2)}) collective-permute-start(f32[2,16,1]{2,1,0:T(8,128)S(1)} %get-tuple-element.115), channel_id=1, source_target_pairs={{1,0},{2,1},{3,2},{0,3},{5,4},{6,5},{7,6},{4,7},{9,8},{10,9},{11,1... | collective-permute-start | bytes 392 | tf_op jit(solution)/shard_map/ppermute | solution.py:21
  231.6 8.3 %collective-permute-start.33 = (f32[1,16,64]{2,1,0:T(8,128)S(1)}, f32[1,16,64]{2,1,0:T(8,128)S(1)}, u32[]{:S(2)}, u32[]{:S(2)}) collective-permute-start(f32[1,16,64]{2,1,0:T(8,128)S(1)} %get-tuple-element.112), channel_id=1, source_target_pairs={{0,8},{4,12},{8,16},{12,20},{16,24},{20,28},{24,32},{28,36},{32,40... | collective-permute-start | bytes 12296 | tf_op jit(solution)/shard_map/ppermute | solution.py:29
  233.5 7.7 %collective-permute-start.34 = (f32[1,16,64]{2,1,0:T(8,128)S(1)}, f32[1,16,64]{2,1,0:T(8,128)S(1)}, u32[]{:S(2)}, u32[]{:S(2)}) collective-permute-start(f32[1,16,64]{2,1,0:T(8,128)S(1)} %get-tuple-element.113), channel_id=1, source_target_pairs={{8,0},{12,4},{16,8},{20,12},{24,16},{28,20},{32,24},{36,28},{40,32... | collective-permute-start | bytes 12296 | tf_op jit(solution)/shard_map/ppermute | solution.py:29
  241.4 11.5 %collective-permute-start.39 = (f32[2,16,1]{2,1,0:T(8,128)S(1)}, f32[2,16,1]{2,1,0:T(8,128)S(1)}, u32[]{:S(2)}, u32[]{:S(2)}) collective-permute-start(f32[2,16,1]{2,1,0:T(8,128)S(1)} %get-tuple-element.108), channel_id=1, source_target_pairs={{0,1},{1,2},{2,3},{3,0},{4,5},{5,6},{6,7},{7,4},{8,9},{9,10},{10,1... | collective-permute-start | bytes 392 | tf_op jit(solution)/shard_map/ppermute | solution.py:20
  241.4 11.5 %collective-permute-start.40 = (f32[2,16,1]{2,1,0:T(8,128)S(1)}, f32[2,16,1]{2,1,0:T(8,128)S(1)}, u32[]{:S(2)}, u32[]{:S(2)}) collective-permute-start(f32[2,16,1]{2,1,0:T(8,128)S(1)} %get-tuple-element.109), channel_id=1, source_target_pairs={{1,0},{2,1},{3,2},{0,3},{5,4},{6,5},{7,6},{4,7},{9,8},{10,9},{11,1... | collective-permute-start | bytes 392 | tf_op jit(solution)/shard_map/ppermute | solution.py:21
  244.6 8.3 %collective-permute-start.37 = (f32[1,16,64]{2,1,0:T(8,128)S(1)}, f32[1,16,64]{2,1,0:T(8,128)S(1)}, u32[]{:S(2)}, u32[]{:S(2)}) collective-permute-start(f32[1,16,64]{2,1,0:T(8,128)S(1)} %get-tuple-element.106), channel_id=1, source_target_pairs={{0,8},{4,12},{8,16},{12,20},{16,24},{20,28},{24,32},{28,36},{32,40... | collective-permute-start | bytes 12296 | tf_op jit(solution)/shard_map/ppermute | solution.py:29
  246.5 7.7 %collective-permute-start.38 = (f32[1,16,64]{2,1,0:T(8,128)S(1)}, f32[1,16,64]{2,1,0:T(8,128)S(1)}, u32[]{:S(2)}, u32[]{:S(2)}) collective-permute-start(f32[1,16,64]{2,1,0:T(8,128)S(1)} %get-tuple-element.107), channel_id=1, source_target_pairs={{8,0},{12,4},{16,8},{20,12},{24,16},{28,20},{32,24},{36,28},{40,32... | collective-permute-start | bytes 12296 | tf_op jit(solution)/shard_map/ppermute | solution.py:29
  254.4 11.5 %collective-permute-start.43 = (f32[2,16,1]{2,1,0:T(8,128)S(1)}, f32[2,16,1]{2,1,0:T(8,128)S(1)}, u32[]{:S(2)}, u32[]{:S(2)}) collective-permute-start(f32[2,16,1]{2,1,0:T(8,128)S(1)} %get-tuple-element.102), channel_id=1, source_target_pairs={{0,1},{1,2},{2,3},{3,0},{4,5},{5,6},{6,7},{7,4},{8,9},{9,10},{10,1... | collective-permute-start | bytes 392 | tf_op jit(solution)/shard_map/ppermute | solution.py:20
  254.4 11.5 %collective-permute-start.44 = (f32[2,16,1]{2,1,0:T(8,128)S(1)}, f32[2,16,1]{2,1,0:T(8,128)S(1)}, u32[]{:S(2)}, u32[]{:S(2)}) collective-permute-start(f32[2,16,1]{2,1,0:T(8,128)S(1)} %get-tuple-element.103), channel_id=1, source_target_pairs={{1,0},{2,1},{3,2},{0,3},{5,4},{6,5},{7,6},{4,7},{9,8},{10,9},{11,1... | collective-permute-start | bytes 392 | tf_op jit(solution)/shard_map/ppermute | solution.py:21
  257.6 8.3 %collective-permute-start.41 = (f32[1,16,64]{2,1,0:T(8,128)S(1)}, f32[1,16,64]{2,1,0:T(8,128)S(1)}, u32[]{:S(2)}, u32[]{:S(2)}) collective-permute-start(f32[1,16,64]{2,1,0:T(8,128)S(1)} %get-tuple-element.100), channel_id=1, source_target_pairs={{0,8},{4,12},{8,16},{12,20},{16,24},{20,28},{24,32},{28,36},{32,40... | collective-permute-start | bytes 12296 | tf_op jit(solution)/shard_map/ppermute | solution.py:29
  259.5 7.7 %collective-permute-start.42 = (f32[1,16,64]{2,1,0:T(8,128)S(1)}, f32[1,16,64]{2,1,0:T(8,128)S(1)}, u32[]{:S(2)}, u32[]{:S(2)}) collective-permute-start(f32[1,16,64]{2,1,0:T(8,128)S(1)} %get-tuple-element.101), channel_id=1, source_target_pairs={{8,0},{12,4},{16,8},{20,12},{24,16},{28,20},{32,24},{36,28},{40,32... | collective-permute-start | bytes 12296 | tf_op jit(solution)/shard_map/ppermute | solution.py:29
  267.6 11.0 %collective-permute-start.47 = (f32[2,32,1]{2,1,0:T(8,128)S(1)}, f32[2,32,1]{2,1,0:T(8,128)S(1)}, u32[]{:S(2)}, u32[]{:S(2)}) collective-permute-start(f32[2,32,1]{2,1,0:T(8,128)S(1)} %get-tuple-element.72), channel_id=1, source_target_pairs={{0,1},{1,2},{2,3},{3,0},{4,5},{5,6},{6,7},{7,4},{8,9},{9,10},{10,1... | collective-permute-start | bytes 776 | tf_op jit(solution)/shard_map/ppermute | solution.py:20
  267.7 10.9 %collective-permute-start.48 = (f32[2,32,1]{2,1,0:T(8,128)S(1)}, f32[2,32,1]{2,1,0:T(8,128)S(1)}, u32[]{:S(2)}, u32[]{:S(2)}) collective-permute-start(f32[2,32,1]{2,1,0:T(8,128)S(1)} %get-tuple-element.73), channel_id=1, source_target_pairs={{1,0},{2,1},{3,2},{0,3},{5,4},{6,5},{7,6},{4,7},{9,8},{10,9},{11,1... | collective-permute-start | bytes 776 | tf_op jit(solution)/shard_map/ppermute | solution.py:21
  270.9 7.7 %collective-permute-start.45 = (f32[1,32,128]{2,1,0:T(8,128)S(1)}, f32[1,32,128]{2,1,0:T(8,128)S(1)}, u32[]{:S(2)}, u32[]{:S(2)}) collective-permute-start(f32[1,32,128]{2,1,0:T(8,128)S(1)} %get-tuple-element.70), channel_id=1, source_target_pairs={{0,4},{4,8},{8,12},{12,16},{16,20},{20,24},{24,28},{28,32},{32,36}... | collective-permute-start | bytes 49160 | tf_op jit(solution)/shard_map/ppermute | solution.py:20
  280.2 11.1 %collective-permute-start.51 = (f32[2,32,1]{2,1,0:T(8,128)S(1)}, f32[2,32,1]{2,1,0:T(8,128)S(1)}, u32[]{:S(2)}, u32[]{:S(2)}) collective-permute-start(f32[2,32,1]{2,1,0:T(8,128)S(1)} %get-tuple-element.66), channel_id=1, source_target_pairs={{0,1},{1,2},{2,3},{3,0},{4,5},{5,6},{6,7},{7,4},{8,9},{9,10},{10,1... | collective-permute-start | bytes 776 | tf_op jit(solution)/shard_map/ppermute | solution.py:20
  280.4 10.9 %collective-permute-start.52 = (f32[2,32,1]{2,1,0:T(8,128)S(1)}, f32[2,32,1]{2,1,0:T(8,128)S(1)}, u32[]{:S(2)}, u32[]{:S(2)}) collective-permute-start(f32[2,32,1]{2,1,0:T(8,128)S(1)} %get-tuple-element.67), channel_id=1, source_target_pairs={{1,0},{2,1},{3,2},{0,3},{5,4},{6,5},{7,6},{4,7},{9,8},{10,9},{11,1... | collective-permute-start | bytes 776 | tf_op jit(solution)/shard_map/ppermute | solution.py:21
  283.6 7.7 %collective-permute-start.49 = (f32[1,32,128]{2,1,0:T(8,128)S(1)}, f32[1,32,128]{2,1,0:T(8,128)S(1)}, u32[]{:S(2)}, u32[]{:S(2)}) collective-permute-start(f32[1,32,128]{2,1,0:T(8,128)S(1)} %get-tuple-element.64), channel_id=1, source_target_pairs={{0,4},{4,8},{8,12},{12,16},{16,20},{20,24},{24,28},{28,32},{32,36}... | collective-permute-start | bytes 49160 | tf_op jit(solution)/shard_map/ppermute | solution.py:20
  293.3 12.6 %collective-permute-start.53 = (f32[1,64,256]{1,2,0:T(8,128)S(1)}, f32[1,64,256]{1,2,0:T(8,128)S(1)}, u32[]{:S(2)}, u32[]{:S(2)}) collective-permute-start(f32[1,64,256]{1,2,0:T(8,128)S(1)} %get-tuple-element.30), channel_id=1, source_target_pairs={{0,4},{4,8},{8,12},{12,16},{16,20},{20,24},{24,28},{28,32},{32,36}... | collective-permute-start | bytes 196616 | tf_op jit(solution)/shard_map/ppermute | solution.py:20
  295.2 10.6 %collective-permute-start.54 = (f32[1,64,256]{1,2,0:T(8,128)S(1)}, f32[1,64,256]{1,2,0:T(8,128)S(1)}, u32[]{:S(2)}, u32[]{:S(2)}) collective-permute-start(f32[1,64,256]{1,2,0:T(8,128)S(1)} %get-tuple-element.31), channel_id=1, source_target_pairs={{4,0},{8,4},{12,8},{16,12},{20,16},{24,20},{28,24},{32,28},{36,32}... | collective-permute-start | bytes 196616 | tf_op jit(solution)/shard_map/ppermute | solution.py:21
  306.9 12.6 %collective-permute-start.57 = (f32[1,64,256]{1,2,0:T(8,128)S(1)}, f32[1,64,256]{1,2,0:T(8,128)S(1)}, u32[]{:S(2)}, u32[]{:S(2)}) collective-permute-start(f32[1,64,256]{1,2,0:T(8,128)S(1)} %get-tuple-element.24), channel_id=1, source_target_pairs={{0,4},{4,8},{8,12},{12,16},{16,20},{20,24},{24,28},{28,32},{32,36}... | collective-permute-start | bytes 196616 | tf_op jit(solution)/shard_map/ppermute | solution.py:20
  308.8 10.6 %collective-permute-start.58 = (f32[1,64,256]{1,2,0:T(8,128)S(1)}, f32[1,64,256]{1,2,0:T(8,128)S(1)}, u32[]{:S(2)}, u32[]{:S(2)}) collective-permute-start(f32[1,64,256]{1,2,0:T(8,128)S(1)} %get-tuple-element.25), channel_id=1, source_target_pairs={{4,0},{8,4},{12,8},{16,12},{20,16},{24,20},{28,24},{32,28},{36,32}... | collective-permute-start | bytes 196616 | tf_op jit(solution)/shard_map/ppermute | solution.py:21
  320.4 13.2 %collective-permute-start.61 = (f32[1,64,256]{1,2,0:T(8,128)S(1)}, f32[1,64,256]{1,2,0:T(8,128)S(1)}, u32[]{:S(2)}, u32[]{:S(2)}) collective-permute-start(f32[1,64,256]{1,2,0:T(8,128)S(1)} %get-tuple-element.18), channel_id=1, source_target_pairs={{0,4},{4,8},{8,12},{12,16},{16,20},{20,24},{24,28},{28,32},{32,36}... | collective-permute-start | bytes 196616 | tf_op jit(solution)/shard_map/ppermute | solution.py:20
  322.3 11.2 %collective-permute-start.62 = (f32[1,64,256]{1,2,0:T(8,128)S(1)}, f32[1,64,256]{1,2,0:T(8,128)S(1)}, u32[]{:S(2)}, u32[]{:S(2)}) collective-permute-start(f32[1,64,256]{1,2,0:T(8,128)S(1)} %get-tuple-element.19), channel_id=1, source_target_pairs={{4,0},{8,4},{12,8},{16,12},{20,16},{24,20},{28,24},{32,28},{36,32}... | collective-permute-start | bytes 196616 | tf_op jit(solution)/shard_map/ppermute | solution.py:21
  (23 other events, 278.0 us)
where the time goes:
time: 342 us; the launch traced here: 337 us
  starting transfers between devices  177 us (52%)
  local copies, waits for them, and re-layouts  96.4 us (28%)
  other arithmetic  44 us (13%)
  waiting for transfers between devices  18.6 us (5%)
    ppermute x28, starting transfers between devices, with_halo(): after = lax.ppermute(leading, axis, down)  114 us
    reshape x4, local copies, waits for them, and re-layouts, coarsen(): values.reshape(depth // 2, 2, width // 2, 2, length // 2, 2)  73.9 us
    ppermute x8, starting transfers between devices, shifted(): return lax.ppermute(block, axis, route)  32.6 us
    reduce_sum x12, other arithmetic, coarsen(): values.reshape(depth // 2, 2, width // 2, 2, length // 2, 2)  31.9 us
    ppermute x28, starting transfers between devices, with_halo(): before = lax.ppermute(last, axis, up)  29.8 us
    unnamed x19, local copies, waits for them, and re-layouts  7.72 us
    ppermute x28, waiting for transfers between devices, with_halo(): after = lax.ppermute(leading, axis, down)  6.93 us
  transfers between devices with their start and end apart: 65, of which 14 were waited for; matrix products, arithmetic and copies ran while one was open for 37% of the time, Pallas kernels for 0%

commit v1 on v0

v1 whole, which is shorter than its diff:
```python
import functools

import jax
import jax.numpy as jnp
from jax import lax
from jax.experimental import pallas as pl
from jax.experimental.pallas import tpu as pltpu
from jax.sharding import PartitionSpec as P

OMEGA = 0.75
MESH = pl.DeviceIdType.MESH

INC = 64
COLS = 256
WIDE = 384
HALO = 3
OWN = 4
TILES = WIDE // 128
LAYERS = OWN + 2 * HALO
FAR = 4


def lane_roll(x, shift):
    return pltpu.roll(x, shift % x.shape[-1], axis=x.ndim - 1)


def row_roll(x, shift):
    return pltpu.roll(x, shift % x.shape[-2], axis=x.ndim - 2)


def iota(shape, dim):
    return lax.broadcasted_iota(jnp.int32, shape, dim)


def beside_fine(v, down, up, w_down, w_up, w_inc, w_raan):
    total = w_down * down + w_up * up
    total = total + w_inc * row_roll(v, 1) + row_roll(w_inc * v, -1)
    return total + w_raan * lane_roll(v, 1) + lane_roll(w_raan * v, -1)


def prev_row(v):
    turned = row_roll(v, 1)
    return jnp.where(iota(v.shape, 0) == 0, lane_roll(turned, 1), turned)


def next_row(v):
    turned = row_roll(v, -1)
    return jnp.where(iota(v.shape, 0) == v.shape[0] - 1, lane_roll(turned, -1), turned)


def coarse_weights(k_alt, k_down, k_up, m_down, m_up, k_inc, k_raan, factor, step):
    half = 0.5 * factor
    lo = half * (k_alt + m_down * k_down)
    hi = half * (k_alt + m_up * k_up)
    outer = (iota(k_inc.shape, 0) == 0) & (iota(k_inc.shape, 1) % 2 == 0)
    w_inc = jnp.where(outer, 0.0, half * (k_inc + prev_row(k_inc)))
    w_raan = half * (k_raan + lane_roll(k_raan, step))
    diagonal = 1.0 + (lo + hi + w_inc + next_row(w_inc) + w_raan + lane_roll(w_raan, -step))
    return m_down * lo, m_up * hi, w_inc, w_raan, diagonal


def beside_coarse(v, down, up, w_down, w_up, w_inc, w_raan, step):
    total = w_down * down + w_up * up
    total = total + w_inc * prev_row(v) + next_row(w_inc * v)
    return total + w_raan * lane_roll(v, step) + lane_roll(w_raan * v, -step)


def kernel(n_alt, n_raan, f_hbm, ka_hbm, ki_hbm, kr_hbm, dens_hbm, sres_hbm,
           ef, eka, eki, ekr, v1, v2, p0, wa, wi, wr, invd, diag, sres,
           pack, rb, xb, tmp, tmp2,
           k2a, k2b, w2, sb4, rb4, rhs2, c2a, c2b, q0, q1, q2, rf,
           k3, w3, r3, c3,
           load_sem, out_sem, send_sem, recv_sem):
    a = lax.axis_index("alt")
    r = lax.axis_index("raan")
    m_lo = jnp.where(a == 0, 0.0, 1.0).astype(jnp.float32)
    m_hi = jnp.where(a == n_alt - 1, 0.0, 1.0).astype(jnp.float32)

    def alt_dev(d):
        return (lax.rem(a + d + n_alt, n_alt), r)

    def raan_dev(d):
        return (a, lax.rem(r + d + n_raan, n_raan))

    count = [0]
    sends = []

    def remote(src, dst, device):
        k = count[0]
        count[0] += 1
        copy = pltpu.make_async_remote_copy(
            src_ref=src, dst_ref=dst, send_sem=send_sem.at[k], recv_sem=recv_sem.at[k],
            device_id=device, device_id_type=MESH)
        copy.start()
        sends.append(copy)
        return copy

    def settle():
        while sends:
            sends.pop().wait_send()

    hbm = (f_hbm, ka_hbm, ki_hbm, kr_hbm)
    ext = (ef, eka, eki, ekr)
    loads = []
    for i in range(4):
        loads.append(pltpu.make_async_copy(
            hbm[i], ext[i].at[HALO:HALO + OWN, :, 0:COLS], load_sem.at[i]))
        loads[i].start()

    barrier = pltpu.get_barrier_semaphore()
    for d in range(1, FAR + 1):
        for side in (d, -d):
            pl.semaphore_signal(barrier, inc=1, device_id=alt_dev(side), device_id_type=MESH)
    for side in (1, -1):
        pl.semaphore_signal(barrier, inc=1, device_id=raan_dev(side), device_id_type=MESH)
    pl.semaphore_wait(barrier, 2 * FAR + 2)

    cols = slice(0, COLS)
    bulk = []
    for i, (up_src, up_dst, down_src, down_dst) in enumerate((
            (slice(2, 4), slice(1, 3), slice(0, 2), slice(7, 9)),
            (slice(2, 4), slice(1, 3), slice(0, 2), slice(7, 9)),
            (slice(3, 4), slice(2, 3), slice(0, 1), slice(7, 8)),
            (slice(3, 4), slice(2, 3), slice(0, 1), slice(7, 8)))):
        bulk.append(remote(hbm[i].at[up_src], ext[i].at[up_dst, :, cols], alt_dev(1)))
        bulk.append(remote(hbm[i].at[down_src], ext[i].at[down_dst, :, cols], alt_dev(-1)))

    quarter = iota((16, 128), 1) // 32
    ring = []
    for i in range(4):
        loads[i].wait()
        for l in range(OWN):
            low = ext[i][HALO + l, :, 0:128]
            high = ext[i][HALO + l, :, 128:256]
            first = low[0:16]
            last = high[0:16]
            for g in range(1, 4):
                first = jnp.where(quarter == g, lane_roll(low[16 * g:16 * g + 16], 32 * g), first)
                last = jnp.where(quarter == (3 + g) % 4, lane_roll(high[16 * g:16 * g + 16], 32 * g), last)
            pack[i, l, 0] = first
            pack[i, l, 1] = last
        ring.append(remote(pack.at[i, :, 0], rb.at[i, :, 0], raan_dev(-1)))
        ring.append(remote(pack.at[i, :, 1], rb.at[i, :, 1], raan_dev(1)))

    def unpack(first, last, dst, layer):
        for g in range(4):
            both = jnp.where(quarter == g, first, last)
            dst[layer, 16 * g:16 * g + 16, COLS:WIDE] = lane_roll(both, -32 * g) if g else both

    for copy in ring:
        copy.wait_recv()
    relay = []
    for i, x_slot, up_src, down_src in (
            (0, slice(0, 2), slice(2, 4), slice(0, 2)),
            (1, slice(2, 4), slice(2, 4), slice(0, 2)),
            (2, slice(4, 5), slice(3, 4), slice(0, 1)),
            (3, slice(5, 6), slice(3, 4), slice(0, 1))):
        relay.append(remote(rb.at[i, up_src], xb.at[0, x_slot], alt_dev(1)))
        relay.append(remote(rb.at[i, down_src], xb.at[1, x_slot], alt_dev(-1)))
    for i in range(4):
        for l in range(OWN):
            unpack(rb[i, l, 0], rb[i, l, 1], ext[i], HALO + l)

    row0 = iota((INC, WIDE), 0) == 0

    def fine_weights(l):
        m_down = jnp.where(l == HALO, m_lo, jnp.where(l == HALO + OWN, m_hi, 1.0))
        m_up = jnp.where(l == HALO - 1, m_lo, jnp.where(l == HALO + OWN - 1, m_hi, 1.0))
        k_alt = eka[l]
        lo = 0.5 * (k_alt + m_down * eka[l - 1])
        hi = 0.5 * (k_alt + m_up * eka[l + 1])
        k_inc = eki[l]
        w_inc = jnp.where(row0, 0.0, 0.5 * (k_inc + row_roll(k_inc, 1)))
        k_raan = ekr[l]
        w_raan = 0.5 * (k_raan + lane_roll(k_raan, 1))
        dg = 1.0 + (lo + hi + w_inc + row_roll(w_inc, -1) + w_raan + lane_roll(w_raan, -1))
        wa[l - 1] = m_down * lo
        wa[l] = m_up * hi
        wi[l] = w_inc
        wr[l] = w_raan
        diag[l] = dg
        invd[l] = OMEGA / dg

    def target_fine(src, l):
        return ef[l] + beside_fine(src[l], src[l - 1], src[l + 1], wa[l - 1], wa[l], wi[l], wr[l])

    def sweep_fine(src, dst, l):
        dst[l] = 0.25 * src[l] + invd[l] * target_fine(src, l)

    def layers(lo, hi, *bodies):
        def body(l, carry):
            for one in bodies:
                one(l)
            return carry
        lax.fori_loop(lo, hi, body, 0)

    first_sweep = functools.partial(sweep_fine, ef, v1)
    layers(4, 6, fine_weights, first_sweep)
    swept = [remote(v1.at[5], v1.at[1], alt_dev(1)), remote(v1.at[4], v1.at[8], alt_dev(-1))]

    even2 = iota((16, WIDE), 1) % 2 == 0

    def row_pairs(scratch, x):
        n = x.shape[0] // 2
        for t in range(TILES):
            scratch[t] = x[:, 128 * t:128 * t + 128]
        return jnp.concatenate(
            [scratch[t, pl.ds(0, n, stride=2)] + scratch[t, pl.ds(1, n, stride=2)] for t in range(TILES)], axis=1)

    def twice(scratch, x):
        n = x.shape[0]
        for t in range(TILES):
            part = x[:, 128 * t:128 * t + 128]
            scratch[t, pl.ds(0, n, stride=2)] = part
            scratch[t, pl.ds(1, n, stride=2)] = part
        return jnp.concatenate([scratch[t] for t in range(TILES)], axis=1)

    def coarsen_fine(total):
        pairs = row_pairs(tmp, total)
        t_a, t_b = pairs[0:16], pairs[16:32]
        return 0.125 * (jnp.where(even2, t_a, t_b) + jnp.where(even2, lane_roll(t_a, -1), lane_roll(t_b, 1)))

    low3 = iota((8, WIDE), 1) % 4 < 2

    def coarsen_mid(total):
        t = row_pairs(tmp2, total)
        return 0.125 * (t + jnp.where(low3, lane_roll(t, -2), lane_roll(t, 2)))

    for j in range(2):
        k2a[2 + j] = coarsen_fine(eka[3 + 2 * j] + eka[4 + 2 * j])
        k2b[2 + j, 0] = coarsen_fine(eki[3 + 2 * j] + eki[4 + 2 * j])
        k2b[2 + j, 1] = coarsen_fine(ekr[3 + 2 * j] + ekr[4 + 2 * j])
    k3[FAR, 0] = coarsen_mid(k2a[2] + k2a[3])
    k3[FAR, 1] = coarsen_mid(k2b[2, 0] + k2b[3, 0])
    k3[FAR, 2] = coarsen_mid(k2b[2, 1] + k2b[3, 1])
    coarse = [
        remote(k2a.at[2:4], k2a.at[0:2], alt_dev(1)), remote(k2a.at[2:4], k2a.at[4:6], alt_dev(-1)),
        remote(k2b.at[3], k2b.at[1], alt_dev(1)), remote(k2b.at[2], k2b.at[4], alt_dev(-1))]

    for copy in bulk + relay:
        copy.wait_recv()
    for side, at in ((0, (1, 2, 2)), (1, (7, 8, 7))):
        for i, slot, layer in ((0, 0, at[0]), (0, 1, at[1]), (1, 2, at[0]), (1, 3, at[1]), (2, 4, at[2]), (3, 5, at[2])):
            unpack(xb[side, slot, 0], xb[side, slot, 1], ext[i], layer)
    layers(2, 4, fine_weights, first_sweep)
    layers(6, 8, fine_weights, first_sweep)
    for copy in swept:
        copy.wait_recv()

    later = []
    for i, x_slot, up_src, up_dst, down_src, down_dst in (
            (1, 6, 1, 0, 2, 9), (2, 7, 2, 1, 1, 8), (3, 8, 2, 1, 1, 8)):
        later.append(remote(hbm[i].at[up_src], ext[i].at[up_dst, :, cols], alt_dev(1)))
        later.append(remote(hbm[i].at[down_src], ext[i].at[down_dst, :, cols], alt_dev(-1)))
        later.append(remote(rb.at[i, up_src], xb.at[0, x_slot], alt_dev(1)))
        later.append(remote(rb.at[i, down_src], xb.at[1, x_slot], alt_dev(-1)))

    layers(2, 8, functools.partial(sweep_fine, v1, v2))

    def residual_fine(l):
        return target_fine(v2, l) - diag[l] * v2[l]

    for copy in coarse:
        copy.wait_recv()
    for x in range(1, 5):
        m_down = {2: m_lo, 4: m_hi}.get(x, 1.0)
        m_up = {1: m_lo, 3: m_hi}.get(x, 1.0)
        w_down, w_up, w_inc, w_raan, dg = coarse_weights(
            k2a[x], k2a[x - 1], k2a[x + 1], m_down, m_up, k2b[x, 0], k2b[x, 1], 0.25, 2)
        for n, value in enumerate((w_down, w_up, w_inc, w_raan, dg, OMEGA / dg)):
            w2[x, n] = value

    for j in range(2):
        rhs2[2 + j] = coarsen_fine(residual_fine(3 + 2 * j) + residual_fine(4 + 2 * j))
        c2a[2 + j] = rhs2[2 + j] * w2[2 + j, 5]
    sb4[0, 0] = rhs2[3]
    sb4[0, 1] = c2a[2]
    sb4[1, 0] = rhs2[2]
    sb4[1, 1] = c2a[3]
    mid = [remote(sb4.at[0], rb4.at[0], alt_dev(1)), remote(sb4.at[1], rb4.at[1], alt_dev(-1))]
    far_k = []
    for d in range(1, FAR + 1):
        for side in (d, -d):
            far_k.append(remote(k3.at[FAR], k3.at[FAR - side], alt_dev(side)))
    dens2 = [remote(v2.at[4:6], v2.at[0:2], alt_dev(1)), remote(v2.at[4:6], v2.at[8:10], alt_dev(-1))]

    for copy in mid:
        copy.wait_recv()
    rhs2[1] = rb4[0, 0]
    c2a[0] = rb4[0, 1]
    rhs2[4] = rb4[1, 0]
    c2a[5] = rb4[1, 1]
    c2a[1] = rhs2[1] * w2[1, 5]
    c2a[4] = rhs2[4] * w2[4, 5]

    def target_mid(src, x):
        return rhs2[x] + beside_coarse(src[x], src[x - 1], src[x + 1], w2[x, 0], w2[x, 1], w2[x, 2], w2[x, 3], 2)

    def sweep_mid(src, dst, x):
        dst[x] = 0.25 * src[x] + w2[x, 5] * target_mid(src, x)

    for x in range(1, 5):
        sweep_mid(c2a, c2b, x)
    residual = [target_mid(c2b, x) - w2[x, 4] * c2b[x] for x in (2, 3)]
    r3[FAR] = coarsen_mid(residual[0] + residual[1])

    for copy in far_k:
        copy.wait_recv()
    for x in range(1, 2 * FAR):
        m_down = jnp.where(lax.rem(a + x - FAR + n_alt, n_alt) == 0, 0.0, 1.0).astype(jnp.float32)
        m_up = jnp.where(lax.rem(a + x - FAR + 1 + n_alt, n_alt) == 0, 0.0, 1.0).astype(jnp.float32)
        w_down, w_up, w_inc, w_raan, dg = coarse_weights(
            k3[x, 0], k3[x - 1, 0], k3[x + 1, 0], m_down, m_up, k3[x, 1], k3[x, 2], 0.0625, 4)
        for n, value in enumerate((w_down, w_up, w_inc, w_raan, OMEGA / dg)):
            w3[x, n] = value
    c3[0, FAR] = r3[FAR] * w3[FAR, 4]
    far = []
    for d in range(1, FAR):
        for side in (d, -d):
            far.append(remote(r3.at[FAR], r3.at[FAR - side], alt_dev(side)))
    for side in (FAR, -FAR):
        far.append(remote(c3.at[0, FAR], c3.at[0, FAR - side], alt_dev(side)))
    ends = [remote(c2b.at[2], c2b.at[0], alt_dev(1)), remote(c2b.at[3], c2b.at[5], alt_dev(-1))]

    for copy in later:
        copy.wait_recv()
    for side, at in ((0, (0, 1)), (1, (9, 8))):
        for i, slot, layer in ((1, 6, at[0]), (2, 7, at[1]), (3, 8, at[1])):
            unpack(xb[side, slot, 0], xb[side, slot, 1], ext[i], layer)
    fine_weights(1)
    fine_weights(8)

    for copy in far:
        copy.wait_recv()
    for x in range(1, 2 * FAR):
        if x != FAR:
            c3[0, x] = r3[x] * w3[x, 4]
    for n in range(3):
        for x in range(1 + n, 2 * FAR - n):
            v = c3[n, x]
            total = r3[x] + beside_coarse(v, c3[n, x - 1], c3[n, x + 1], w3[x, 0], w3[x, 1], w3[x, 2], w3[x, 3], 4)
            c3[n + 1, x] = 0.25 * v + w3[x, 4] * total

    for copy in ends:
        copy.wait_recv()
    for j in range(3):
        part = twice(tmp2, c3[3, FAR - 1 + j])
        for x in (2 * j, 2 * j + 1):
            q0[x] = c2b[x] + part
    for x in range(1, 5):
        sweep_mid(q0, q1, x)
    for x in (2, 3):
        sweep_mid(q1, q2, x)
    up2 = [remote(q2.at[2:4], q2.at[0:2], alt_dev(1)), remote(q2.at[2:4], q2.at[4:6], alt_dev(-1))]

    def refine_mid(x):
        c = q2[x]
        part_a = jnp.where(even2, c, lane_roll(c, 1))
        part_b = jnp.where(even2, lane_roll(c, -1), c)
        rf[x] = twice(tmp, jnp.concatenate([part_a, part_b], axis=0))

    def correct(l):
        p0[l] = v2[l] + rf[(l - 1) // 2 + 1 if l else 0]

    for x in (2, 3):
        refine_mid(x)
    for l in range(HALO, HALO + OWN):
        correct(l)
    for copy in dens2:
        copy.wait_recv()
    settle_now = list(sends)
    sends.clear()
    for copy in settle_now:
        copy.wait_send()
    last_sweep = functools.partial(sweep_fine, p0, v1)
    layers(4, 6, last_sweep)
    for copy in up2:
        copy.wait_recv()
    for x in (0, 1, 4, 5):
        refine_mid(x)
    for l in (0, 1, 2, 7, 8, 9):
        correct(l)
    layers(1, 4, last_sweep)
    layers(6, 9, last_sweep)
    layers(2, 8, functools.partial(sweep_fine, v1, v2))
    outs = [pltpu.make_async_copy(v2.at[HALO:HALO + OWN, :, cols], dens_hbm, out_sem.at[0])]
    outs[0].start()

    def last_residual(l):
        value = (1.0 / OMEGA) * (invd[l] * target_fine(v2, l)) - v2[l]
        sres[l - HALO] = value[:, 0:COLS]

    layers(HALO, HALO + OWN, last_residual)
    outs.append(pltpu.make_async_copy(sres, sres_hbm, out_sem.at[1]))
    outs[1].start()
    settle()
    for copy in outs:
        copy.wait()


def solution(mesh):
    n_alt, n_raan = mesh.shape["alt"], mesh.shape["raan"]
    spec = P("alt", None, "raan")
    anywhere = pl.BlockSpec(memory_space=pl.ANY)

    def vmem(*shape):
        return pltpu.VMEM(shape, jnp.float32)

    def shards(source, k_alt, k_inc, k_raan):
        big = [vmem(LAYERS, INC, WIDE)] * 12
        scratch = big + [vmem(OWN, INC, COLS)]
        scratch += [vmem(4, OWN, 2, 16, 128), vmem(4, OWN, 2, 16, 128), vmem(2, 9, 2, 16, 128),
                    vmem(TILES, INC, 128), vmem(TILES, 16, 128)]
        scratch += [vmem(6, 16, WIDE), vmem(6, 2, 16, WIDE), vmem(6, 6, 16, WIDE), vmem(2, 2, 16, WIDE),
                    vmem(2, 2, 16, WIDE)] + [vmem(6, 16, WIDE)] * 6 + [vmem(6, INC, WIDE)]
        scratch += [vmem(2 * FAR + 1, 3, 8, WIDE), vmem(2 * FAR + 1, 5, 8, WIDE), vmem(2 * FAR + 1, 8, WIDE),
                    vmem(4, 2 * FAR + 1, 8, WIDE)]
        scratch += [pltpu.SemaphoreType.DMA((4,)), pltpu.SemaphoreType.DMA((2,)),
                    pltpu.SemaphoreType.DMA((72,)), pltpu.SemaphoreType.DMA((72,))]
        shape = jax.ShapeDtypeStruct(source.shape, source.dtype)
        return pl.pallas_call(
            functools.partial(kernel, n_alt, n_raan),
            out_shape=(shape, shape),
            in_specs=[anywhere] * 4,
            out_specs=(anywhere, anywhere),
            scratch_shapes=scratch,
            compiler_params=pltpu.CompilerParams(
                collective_id=0, has_side_effects=True, vmem_limit_bytes=48 * 1024 * 1024),
            name="vcycle",
        )(source, k_alt, k_inc, k_raan)

    return jax.shard_map(shards, mesh=mesh, in_specs=(spec,) * 4, out_specs=(spec, spec), check_vma=False)
```

time: 342 us -> 48.8 us (0.14)
  the two profiles are of different devices: /device:TPU:24 before, /device:TPU:1 now
where the time goes in v1:
time: 48.8 us; the launch traced here: 48.6 us
  Pallas kernels  42.7 us (88%)
  local copies, waits for them, and re-layouts  5.2 us (11%)
  between operations  0.65 us (1%)
    pallas_call x1, Pallas kernels, shards(): pl.pallas_call(functools.partial(kernel, n_alt, n_raan), out_shape=(shape...  42.7 us
    unnamed x10, local copies, waits for them, and re-layouts  5.2 us

profile of v1, /device:TPU:1, one launch (start us, length us, event | category | flops | bytes accessed | tf_op | source)
XLA Modules:
  0.0 48.6 jit_solution(17946291517024808876)
XLA Ops:
  0.6 0.0 copy-start
  0.6 0.9 %copy-done = f32[4,64,256]{2,1,0:T(8,128)S(1)} copy-done((f32[4,64,256]{2,1,0:T(8,128)S(1)}, f32[4,64,256]{2,1,0:T(8,128)}, u32[]{:S(2)}) %copy-start) | copy-done | bytes 262168
  1.6 0.0 copy-start.1
  1.6 0.9 %copy-done.1 = f32[4,64,256]{2,1,0:T(8,128)S(1)} copy-done((f32[4,64,256]{2,1,0:T(8,128)S(1)}, f32[4,64,256]{2,1,0:T(8,128)}, u32[]{:S(2)}) %copy-start.1) | copy-done | bytes 262168
  2.5 0.0 copy-start.2
  2.5 0.9 %copy-done.2 = f32[4,64,256]{2,1,0:T(8,128)S(1)} copy-done((f32[4,64,256]{2,1,0:T(8,128)S(1)}, f32[4,64,256]{2,1,0:T(8,128)}, u32[]{:S(2)}) %copy-start.2) | copy-done | bytes 262168
  3.5 0.0 copy-start.3
  3.5 0.9 %copy-done.3 = f32[4,64,256]{2,1,0:T(8,128)S(1)} copy-done((f32[4,64,256]{2,1,0:T(8,128)S(1)}, f32[4,64,256]{2,1,0:T(8,128)}, u32[]{:S(2)}) %copy-start.3) | copy-done | bytes 262168
  4.4 42.7 %vcycle.1 = (f32[4,64,256]{2,1,0:T(8,128)S(1)}, f32[4,64,256]{2,1,0:T(8,128)S(1)}) custom-call(f32[4,64,256]{2,1,0:T(8,128)S(1)} %copy-done, f32[4,64,256]{2,1,0:T(8,128)S(1)} %copy-done.1, f32[4,64,256]{2,1,0:T(8,128)S(1)} %copy-done.2, f32[4,64,256]{2,1,0:T(8,128)S(1)} %copy-done.3), custom_call_target="tpu_custom_call" | custom-call | tf_op jit(solution)/shard_map/vcycle/pallas_call | solution.py:421
  47.2 0.7 %copy.8 = f32[4,64,256]{2,1,0:T(8,128)} copy(f32[4,64,256]{2,1,0:T(8,128)S(1)} %get-tuple-element.4) | data formatting | bytes 524288
  47.9 0.7 %copy.9 = f32[4,64,256]{2,1,0:T(8,128)} copy(f32[4,64,256]{2,1,0:T(8,128)S(1)} %get-tuple-element.5) | data formatting | bytes 524288
Async XLA Ops:
  0.6 1.0 %copy-start = (f32[4,64,256]{2,1,0:T(8,128)S(1)}, f32[4,64,256]{2,1,0:T(8,128)}, u32[]{:S(2)}) copy-start(f32[4,64,256]{2,1,0:T(8,128)} %f_hbm.1) | copy-start | bytes 786436
  1.6 0.9 %copy-start.1 = (f32[4,64,256]{2,1,0:T(8,128)S(1)}, f32[4,64,256]{2,1,0:T(8,128)}, u32[]{:S(2)}) copy-start(f32[4,64,256]{2,1,0:T(8,128)} %ka_hbm.1) | copy-start | bytes 786436
  2.5 0.9 %copy-start.2 = (f32[4,64,256]{2,1,0:T(8,128)S(1)}, f32[4,64,256]{2,1,0:T(8,128)}, u32[]{:S(2)}) copy-start(f32[4,64,256]{2,1,0:T(8,128)} %ki_hbm.1) | copy-start | bytes 786436
  3.5 0.9 %copy-start.3 = (f32[4,64,256]{2,1,0:T(8,128)S(1)}, f32[4,64,256]{2,1,0:T(8,128)}, u32[]{:S(2)}) copy-start(f32[4,64,256]{2,1,0:T(8,128)} %kr_hbm.1) | copy-start | bytes 786436

commit v2 on v1

v2 whole, which is shorter than its diff:
```python
import functools

import jax
import jax.numpy as jnp
from jax import lax
from jax.experimental import pallas as pl
from jax.experimental.pallas import tpu as pltpu
from jax.sharding import PartitionSpec as P

OMEGA = 0.75
MESH = pl.DeviceIdType.MESH

INC = 64
COLS = 256
WIDE = 384
HALO = 2
OWN = 4
TILES = WIDE // 128
LAYERS = OWN + 2 * HALO
FAR = 4


def lane_roll(x, shift):
    return pltpu.roll(x, shift % x.shape[-1], axis=x.ndim - 1)


def row_roll(x, shift):
    return pltpu.roll(x, shift % x.shape[-2], axis=x.ndim - 2)


def iota(shape, dim):
    return lax.broadcasted_iota(jnp.int32, shape, dim)


def beside_fine(v, down, up, w_down, w_up, w_inc, w_raan):
    total = w_down * down + w_up * up
    total = total + w_inc * row_roll(v, 1) + row_roll(w_inc * v, -1)
    return total + w_raan * lane_roll(v, 1) + lane_roll(w_raan * v, -1)


def prev_row(v):
    turned = row_roll(v, 1)
    return jnp.where(iota(v.shape, 0) == 0, lane_roll(turned, 1), turned)


def next_row(v):
    turned = row_roll(v, -1)
    return jnp.where(iota(v.shape, 0) == v.shape[0] - 1, lane_roll(turned, -1), turned)


def coarse_weights(k_alt, k_down, k_up, m_down, m_up, k_inc, k_raan, factor, step):
    half = 0.5 * factor
    lo = half * (k_alt + m_down * k_down)
    hi = half * (k_alt + m_up * k_up)
    outer = (iota(k_inc.shape, 0) == 0) & (iota(k_inc.shape, 1) % 2 == 0)
    w_inc = jnp.where(outer, 0.0, half * (k_inc + prev_row(k_inc)))
    w_raan = half * (k_raan + lane_roll(k_raan, step))
    diagonal = 1.0 + (lo + hi + w_inc + next_row(w_inc) + w_raan + lane_roll(w_raan, -step))
    return m_down * lo, m_up * hi, w_inc, w_raan, diagonal


def beside_coarse(v, down, up, w_down, w_up, w_inc, w_raan, step):
    total = w_down * down + w_up * up
    total = total + w_inc * prev_row(v) + next_row(w_inc * v)
    return total + w_raan * lane_roll(v, step) + lane_roll(w_raan * v, -step)


class Exchange:
    def __init__(self, ups, downs, distance, has_up, has_down):
        self.ups, self.downs = ups, downs
        self.has_up, self.has_down = has_up(distance), has_down(distance)

    def start(self):
        @pl.when(self.has_up)
        def _():
            for copy in self.ups:
                copy.start()

        @pl.when(self.has_down)
        def _():
            for copy in self.downs:
                copy.start()

    def wait_recv(self):
        @pl.when(self.has_down)
        def _():
            for copy in self.ups:
                copy.wait_recv()

        @pl.when(self.has_up)
        def _():
            for copy in self.downs:
                copy.wait_recv()

    def wait_send(self):
        @pl.when(self.has_up)
        def _():
            for copy in self.ups:
                copy.wait_send()

        @pl.when(self.has_down)
        def _():
            for copy in self.downs:
                copy.wait_send()


def kernel(n_alt, n_raan, f_hbm, ka_hbm, ki_hbm, kr_hbm, dens_hbm, sres_hbm,
           ef, eka, eki, ekr, v1, v2, p0, p1, p2, wa, wi, wr, invd, diag, sres,
           pack, rb, xb, tmp, tmp2,
           k2a, k2b, w2, sb4, rb4, rhs2, c2a, c2b, q0, q1, q2, rf,
           k3, w3, r3, c3, s3, l3,
           load_sem, out_sem, send_sem, recv_sem, near):
    a = lax.axis_index("alt")
    r = lax.axis_index("raan")
    m_lo = jnp.where(a == 0, 0.0, 1.0).astype(jnp.float32)
    m_hi = jnp.where(a == n_alt - 1, 0.0, 1.0).astype(jnp.float32)

    def has_up(d):
        return a < n_alt - d

    def has_down(d):
        return a >= d

    def alt_dev(d):
        return (lax.rem(a + d + n_alt, n_alt), r)

    def raan_dev(d):
        return (a, lax.rem(r + d + n_raan, n_raan))

    count = [0]
    sends = []

    def describe(src, dst, device):
        k = count[0]
        count[0] += 1
        return pltpu.make_async_remote_copy(
            src_ref=src, dst_ref=dst, send_sem=send_sem.at[k], recv_sem=recv_sem.at[k],
            device_id=device, device_id_type=MESH)

    def remote(src, dst, device):
        copy = describe(src, dst, device)
        copy.start()
        sends.append(copy)
        return copy

    def exchange(ups, downs, distance=1):
        copy = Exchange([describe(s, d, alt_dev(distance)) for s, d in ups],
                        [describe(s, d, alt_dev(-distance)) for s, d in downs], distance, has_up, has_down)
        copy.start()
        sends.append(copy)
        return copy

    hbm = (f_hbm, ka_hbm, ki_hbm, kr_hbm)
    ext = (ef, eka, eki, ekr)
    cols = slice(0, COLS)
    own = slice(HALO, HALO + OWN)
    loads = []
    for i in range(4):
        loads.append(pltpu.make_async_copy(hbm[i], ext[i].at[own, :, cols], load_sem.at[i]))

    barrier = pltpu.get_barrier_semaphore()

    def greet(sem_up, sem_down):
        @pl.when(has_up(1))
        def _():
            pl.semaphore_signal(sem_up, inc=1, device_id=alt_dev(1), device_id_type=MESH)

        @pl.when(has_down(1))
        def _():
            pl.semaphore_signal(sem_down, inc=1, device_id=alt_dev(-1), device_id_type=MESH)

    greet(barrier, barrier)
    for side in (1, -1):
        pl.semaphore_signal(barrier, inc=1, device_id=raan_dev(side), device_id_type=MESH)
    for i in range(4):
        loads[i].start()

    @pl.when(a == 0)
    def _():
        for ref in (ef, eka, eki, ekr, v1, v2, p1):
            ref[0:HALO] = jnp.zeros((HALO, INC, WIDE), jnp.float32)
        xb[0] = jnp.zeros(xb.shape[1:], jnp.float32)
        rb4[0] = jnp.zeros(rb4.shape[1:], jnp.float32)
        for ref in (k2a, k2b, c2b, q2):
            ref[0:2] = jnp.zeros((2,) + ref.shape[1:], jnp.float32)

    @pl.when(a == n_alt - 1)
    def _():
        for ref in (ef, eka, eki, ekr, v1, v2, p1):
            ref[HALO + OWN:LAYERS] = jnp.zeros((HALO, INC, WIDE), jnp.float32)
        xb[1] = jnp.zeros(xb.shape[1:], jnp.float32)
        rb4[1] = jnp.zeros(rb4.shape[1:], jnp.float32)
        for ref in (k2a, k2b, c2b, q2):
            ref[4:6] = jnp.zeros((2,) + ref.shape[1:], jnp.float32)

    for d in range(1, FAR + 1):
        for side, here in ((d, has_up(d)), (-d, has_down(d))):
            @pl.when(jnp.logical_not(here))
            def _():
                l3[:, FAR + side] = jnp.zeros((2, 8, WIDE), jnp.float32)

    pl.semaphore_wait(barrier, 2 + has_up(1).astype(jnp.int32) + has_down(1).astype(jnp.int32))

    low2, high2, low1, high1 = slice(0, 2), slice(2, 4), slice(0, 1), slice(3, 4)
    below2, above2, below1, above1 = slice(0, 2), slice(6, 8), slice(1, 2), slice(6, 7)
    bulk = exchange(
        [(hbm[i].at[high2 if i < 2 else high1], ext[i].at[below2 if i < 2 else below1, :, cols]) for i in range(4)],
        [(hbm[i].at[low2 if i < 2 else low1], ext[i].at[above2 if i < 2 else above1, :, cols]) for i in range(4)])

    quarter = iota((16, 128), 1) // 32
    ring = []
    for i in range(4):
        loads[i].wait()
        for l in range(OWN):
            low = ext[i][HALO + l, :, 0:128]
            high = ext[i][HALO + l, :, 128:256]
            first = low[0:16]
            last = high[0:16]
            for g in range(1, 4):
                first = jnp.where(quarter == g, lane_roll(low[16 * g:16 * g + 16], 32 * g), first)
                last = jnp.where(quarter == (3 + g) % 4, lane_roll(high[16 * g:16 * g + 16], 32 * g), last)
            pack[i, l, 0] = first
            pack[i, l, 1] = last
        ring.append((remote(pack.at[i, :, 0], rb.at[i, :, 0], raan_dev(-1)),
                     remote(pack.at[i, :, 1], rb.at[i, :, 1], raan_dev(1))))

    greet(near.at[0, 0], near.at[0, 1])

    def unpack(first, last, dst, layer):
        for g in range(4):
            both = jnp.where(quarter == g, first, last)
            dst[layer, 16 * g:16 * g + 16, COLS:WIDE] = lane_roll(both, -32 * g) if g else both

    relay = []
    x_slot = (slice(0, 2), slice(2, 4), slice(4, 5), slice(5, 6))
    for i in range(4):
        for copy in ring[i]:
            copy.wait_recv()
        relay.append(exchange([(rb.at[i, high2 if i < 2 else high1], xb.at[0, x_slot[i]])],
                              [(rb.at[i, low2 if i < 2 else low1], xb.at[1, x_slot[i]])]))
        for l in range(OWN):
            unpack(rb[i, l, 0], rb[i, l, 1], ext[i], HALO + l)

    row0 = iota((INC, WIDE), 0) == 0

    def fine_weights(l):
        m_down = jnp.where(l == HALO, m_lo, jnp.where(l == HALO + OWN, m_hi, 1.0))
        m_up = jnp.where(l == HALO - 1, m_lo, jnp.where(l == HALO + OWN - 1, m_hi, 1.0))
        k_alt = eka[l]
        lo = 0.5 * (k_alt + m_down * eka[l - 1])
        hi = 0.5 * (k_alt + m_up * eka[l + 1])
        k_inc = eki[l]
        w_inc = jnp.where(row0, 0.0, 0.5 * (k_inc + row_roll(k_inc, 1)))
        k_raan = ekr[l]
        w_raan = 0.5 * (k_raan + lane_roll(k_raan, 1))
        dg = 1.0 + (lo + hi + w_inc + row_roll(w_inc, -1) + w_raan + lane_roll(w_raan, -1))
        wa[l - 1] = m_down * lo
        wa[l] = m_up * hi
        wi[l] = w_inc
        wr[l] = w_raan
        diag[l] = dg
        invd[l] = OMEGA / dg

    def target_fine(src, l):
        return ef[l] + beside_fine(src[l], src[l - 1], src[l + 1], wa[l - 1], wa[l], wi[l], wr[l])

    def sweep_fine(src, dst, l):
        dst[l] = 0.25 * src[l] + invd[l] * target_fine(src, l)

    def layers(lo, hi, *bodies):
        def body(l, carry):
            for one in bodies:
                one(l)
            return carry
        lax.fori_loop(lo, hi, body, 0)

    first_sweep = functools.partial(sweep_fine, ef, v1)
    layers(3, 5, fine_weights, first_sweep)
    swept = exchange([(v1.at[4], v1.at[0])], [(v1.at[3], v1.at[7])])

    even2 = iota((16, WIDE), 1) % 2 == 0

    def row_pairs(scratch, x):
        n = x.shape[0] // 2
        for t in range(TILES):
            scratch[t] = x[:, 128 * t:128 * t + 128]
        return jnp.concatenate(
            [scratch[t, pl.ds(0, n, stride=2)] + scratch[t, pl.ds(1, n, stride=2)] for t in range(TILES)], axis=1)

    def twice(scratch, x):
        n = x.shape[0]
        for t in range(TILES):
            part = x[:, 128 * t:128 * t + 128]
            scratch[t, pl.ds(0, n, stride=2)] = part
            scratch[t, pl.ds(1, n, stride=2)] = part
        return jnp.concatenate([scratch[t] for t in range(TILES)], axis=1)

    def coarsen_fine(total):
        pairs = row_pairs(tmp, total)
        t_a, t_b = pairs[0:16], pairs[16:32]
        return 0.125 * (jnp.where(even2, t_a, t_b) + jnp.where(even2, lane_roll(t_a, -1), lane_roll(t_b, 1)))

    low3 = iota((8, WIDE), 1) % 4 < 2

    def coarsen_mid(total):
        t = row_pairs(tmp2, total)
        return 0.125 * (t + jnp.where(low3, lane_roll(t, -2), lane_roll(t, 2)))

    def first_of(pair):
        return jnp.where(low3, pair, lane_roll(pair, 2))

    def second_of(pair):
        return jnp.where(low3, lane_roll(pair, -2), pair)

    for j in range(2):
        k2a[2 + j] = coarsen_fine(eka[2 + 2 * j] + eka[3 + 2 * j])
        k2b[2 + j, 0] = coarsen_fine(eki[2 + 2 * j] + eki[3 + 2 * j])
        k2b[2 + j, 1] = coarsen_fine(ekr[2 + 2 * j] + ekr[3 + 2 * j])
    k3[FAR, 0] = coarsen_mid(k2a[2] + k2a[3])
    k3[FAR, 1] = coarsen_mid(k2b[2, 0] + k2b[3, 0])
    k3[FAR, 2] = coarsen_mid(k2b[2, 1] + k2b[3, 1])
    coarse = exchange([(k2a.at[2:4], k2a.at[0:2]), (k2b.at[3], k2b.at[1])],
                      [(k2a.at[2:4], k2a.at[4:6]), (k2b.at[2], k2b.at[4])])

    def hear(step):
        @pl.when(has_down(1))
        def _():
            pl.semaphore_wait(near.at[step, 0], 1)

        @pl.when(has_up(1))
        def _():
            pl.semaphore_wait(near.at[step, 1], 1)

    for step in range(2):
        hear(step)
        greet(near.at[step + 1, 0], near.at[step + 1, 1])

    bulk.wait_recv()
    for copy in relay:
        copy.wait_recv()
    for side, two, one in ((0, (0, 1), 1), (1, (6, 7), 6)):
        for i, slot, layer in ((0, 0, two[0]), (0, 1, two[1]), (1, 2, two[0]), (1, 3, two[1]), (2, 4, one), (3, 5, one)):
            unpack(xb[side, slot, 0], xb[side, slot, 1], ext[i], layer)
    layers(1, 3, fine_weights, first_sweep)
    layers(5, 7, fine_weights, first_sweep)

    hear(2)
    s3[0] = jnp.where(low3, k3[FAR, 0], k3[FAR, 1])
    far_k = []
    for d in range(1, FAR + 1):
        far_k.append(exchange([(s3.at[0], l3.at[0, FAR - d])], [(s3.at[0], l3.at[0, FAR + d])], d))

    coarse.wait_recv()
    for x in range(1, 5):
        m_down = {2: m_lo, 4: m_hi}.get(x, 1.0)
        m_up = {1: m_lo, 3: m_hi}.get(x, 1.0)
        w_down, w_up, w_inc, w_raan, dg = coarse_weights(
            k2a[x], k2a[x - 1], k2a[x + 1], m_down, m_up, k2b[x, 0], k2b[x, 1], 0.25, 2)
        for n, value in enumerate((w_down, w_up, w_inc, w_raan, dg, OMEGA / dg)):
            w2[x, n] = value

    swept.wait_recv()
    layers(1, 7, functools.partial(sweep_fine, v1, v2))

    def residual_fine(l):
        return target_fine(v2, l) - diag[l] * v2[l]

    for j in range(2):
        rhs2[2 + j] = coarsen_fine(residual_fine(2 + 2 * j) + residual_fine(3 + 2 * j))
        c2a[2 + j] = rhs2[2 + j] * w2[2 + j, 5]
    sb4[0, 0] = rhs2[3]
    sb4[0, 1] = c2a[2]
    sb4[1, 0] = rhs2[2]
    sb4[1, 1] = c2a[3]
    mid = exchange([(sb4.at[0], rb4.at[0])], [(sb4.at[1], rb4.at[1])])
    dens2 = exchange([(v2.at[4], v2.at[0])], [(v2.at[3], v2.at[7])])

    for copy in far_k:
        copy.wait_recv()
    for x in range(2 * FAR + 1):
        if x != FAR:
            k3[x, 0] = first_of(l3[0, x])
            k3[x, 1] = second_of(l3[0, x])

    def weights_far(x):
        at = a + x - FAR
        m_down = jnp.where(at == 0, 0.0, 1.0).astype(jnp.float32)
        m_up = jnp.where(at == n_alt - 1, 0.0, 1.0).astype(jnp.float32)
        w_down, w_up, w_inc, w_raan, dg = coarse_weights(
            k3[x, 0], k3[x - 1, 0], k3[x + 1, 0], m_down, m_up, k3[x, 1], k3[x, 2], 0.0625, 4)
        for n, value in enumerate((w_down, w_up, w_inc, w_raan, OMEGA / dg)):
            w3[x, n] = value

    weights_far(FAR)

    mid.wait_recv()
    rhs2[1] = rb4[0, 0]
    c2a[0] = rb4[0, 1]
    rhs2[4] = rb4[1, 0]
    c2a[5] = rb4[1, 1]
    c2a[1] = rhs2[1] * w2[1, 5]
    c2a[4] = rhs2[4] * w2[4, 5]

    def target_mid(src, x):
        return rhs2[x] + beside_coarse(src[x], src[x - 1], src[x + 1], w2[x, 0], w2[x, 1], w2[x, 2], w2[x, 3], 2)

    def sweep_mid(src, dst, x):
        dst[x] = 0.25 * src[x] + w2[x, 5] * target_mid(src, x)

    for x in range(1, 5):
        sweep_mid(c2a, c2b, x)
    residual = [target_mid(c2b, x) - w2[x, 4] * c2b[x] for x in (2, 3)]
    r3[FAR] = coarsen_mid(residual[0] + residual[1])
    c3[0, FAR] = r3[FAR] * w3[FAR, 4]
    s3[1] = jnp.where(low3, r3[FAR], k3[FAR, 2])
    s3[2] = c3[0, FAR]
    far = []
    for d in range(FAR, 0, -1):
        part = s3.at[1 if d < FAR else 2]
        far.append(exchange([(part, l3.at[1, FAR - d])], [(part, l3.at[1, FAR + d])], d))
    ends = exchange([(c2b.at[2], c2b.at[0])], [(c2b.at[3], c2b.at[5])])

    for copy in far:
        copy.wait_recv()
    for x in range(1, 2 * FAR):
        if x != FAR:
            r3[x] = first_of(l3[1, x])
            k3[x, 2] = second_of(l3[1, x])
            weights_far(x)
            c3[0, x] = r3[x] * w3[x, 4]
    for x in (0, 2 * FAR):
        c3[0, x] = l3[1, x]
    for n in range(3):
        for x in range(1 + n, 2 * FAR - n):
            v = c3[n, x]
            total = r3[x] + beside_coarse(v, c3[n, x - 1], c3[n, x + 1], w3[x, 0], w3[x, 1], w3[x, 2], w3[x, 3], 4)
            c3[n + 1, x] = 0.25 * v + w3[x, 4] * total

    ends.wait_recv()
    for j in range(3):
        part = twice(tmp2, c3[3, FAR - 1 + j])
        for x in (2 * j, 2 * j + 1):
            q0[x] = c2b[x] + part
    for x in range(1, 5):
        sweep_mid(q0, q1, x)
    for x in (2, 3):
        sweep_mid(q1, q2, x)
    up2 = exchange([(q2.at[3], q2.at[1])], [(q2.at[2], q2.at[4])])

    def refine_mid(x):
        c = q2[x]
        part_a = jnp.where(even2, c, lane_roll(c, 1))
        part_b = jnp.where(even2, lane_roll(c, -1), c)
        rf[x] = twice(tmp, jnp.concatenate([part_a, part_b], axis=0))

    def correct(x):
        refine_mid(x)
        for l in (2 * x - 2, 2 * x - 1):
            p0[l] = v2[l] + rf[x]

    correct(2)
    correct(3)
    last_sweep = functools.partial(sweep_fine, p0, p1)
    layers(3, 5, last_sweep)
    inner = exchange([(p1.at[4], p1.at[0])], [(p1.at[3], p1.at[7])])
    dens2.wait_recv()
    up2.wait_recv()
    correct(1)
    correct(4)
    layers(1, 3, last_sweep)
    layers(5, 7, last_sweep)
    layers(2, 6, functools.partial(sweep_fine, p1, p2))
    outs = [pltpu.make_async_copy(p2.at[own, :, cols], dens_hbm, out_sem.at[0])]
    outs[0].start()

    def last_residual(l):
        value = (1.0 / OMEGA) * (invd[l] * target_fine(p2, l)) - p2[l]
        sres[l - HALO] = value[:, 0:COLS]

    layers(3, 5, last_residual)
    inner.wait_recv()
    sweep_fine(p1, p2, 1)
    sweep_fine(p1, p2, 6)
    last_residual(2)
    last_residual(5)
    outs.append(pltpu.make_async_copy(sres, sres_hbm, out_sem.at[1]))
    outs[1].start()
    for copy in sends:
        copy.wait_send()
    for copy in outs:
        copy.wait()


def solution(mesh):
    n_alt, n_raan = mesh.shape["alt"], mesh.shape["raan"]
    spec = P("alt", None, "raan")
    anywhere = pl.BlockSpec(memory_space=pl.ANY)

    def vmem(*shape):
        return pltpu.VMEM(shape, jnp.float32)

    def shards(source, k_alt, k_inc, k_raan):
        scratch = [vmem(LAYERS, INC, WIDE)] * 14 + [vmem(OWN, INC, COLS)]
        scratch += [vmem(4, OWN, 2, 16, 128), vmem(4, OWN, 2, 16, 128), vmem(2, 6, 2, 16, 128),
                    vmem(TILES, INC, 128), vmem(TILES, 16, 128)]
        scratch += [vmem(6, 16, WIDE), vmem(6, 2, 16, WIDE), vmem(6, 6, 16, WIDE), vmem(2, 2, 16, WIDE),
                    vmem(2, 2, 16, WIDE)] + [vmem(6, 16, WIDE)] * 6 + [vmem(6, INC, WIDE)]
        scratch += [vmem(2 * FAR + 1, 3, 8, WIDE), vmem(2 * FAR + 1, 5, 8, WIDE), vmem(2 * FAR + 1, 8, WIDE),
                    vmem(4, 2 * FAR + 1, 8, WIDE), vmem(3, 8, WIDE), vmem(2, 2 * FAR + 1, 8, WIDE)]
        scratch += [pltpu.SemaphoreType.DMA((4,)), pltpu.SemaphoreType.DMA((2,)),
                    pltpu.SemaphoreType.DMA((64,)), pltpu.SemaphoreType.DMA((64,)),
                    pltpu.SemaphoreType.REGULAR((3, 2))]
        shape = jax.ShapeDtypeStruct(source.shape, source.dtype)
        return pl.pallas_call(
            functools.partial(kernel, n_alt, n_raan),
            out_shape=(shape, shape),
            in_specs=[pl.BlockSpec(memory_space=pltpu.HBM)] * 4,
            out_specs=(anywhere, anywhere),
            scratch_shapes=scratch,
            compiler_params=pltpu.CompilerParams(
                collective_id=0, has_side_effects=True, vmem_limit_bytes=64 * 1024 * 1024 - 512 * 1024),
            name="vcycle",
        )(source, k_alt, k_inc, k_raan)

    return jax.shard_map(shards, mesh=mesh, in_specs=(spec,) * 4, out_specs=(spec, spec), check_vma=False)
```

time: 48.8 us -> 38.6 us (0.79)
  the two profiles are of different devices: /device:TPU:1 before, /device:TPU:24 now
where the time goes in v2:
time: 38.6 us; the launch traced here: 38.5 us
  Pallas kernels  35.5 us (92%)
  local copies, waits for them, and re-layouts  2.42 us (6%)
  between operations  0.65 us (2%)
    pallas_call x1, Pallas kernels, shards(): pl.pallas_call(functools.partial(kernel, n_alt, n_raan), out_shape=(shape...  35.5 us
    unnamed x4, local copies, waits for them, and re-layouts  2.42 us

profile of v2, /device:TPU:24, one launch (start us, length us, event | category | flops | bytes accessed | tf_op | source)
XLA Modules:
  0.0 38.5 jit_solution(6335198826244298970)
XLA Ops:
  0.6 35.5 %vcycle.1 = (f32[4,64,256]{2,1,0:T(8,128)}, f32[4,64,256]{2,1,0:T(8,128)}) custom-call(f32[4,64,256]{2,1,0:T(8,128)} %f_hbm.1, f32[4,64,256]{2,1,0:T(8,128)} %ka_hbm.1, f32[4,64,256]{2,1,0:T(8,128)} %ki_hbm.1, f32[4,64,256]{2,1,0:T(8,128)} %kr_hbm.1), custom_call_target="tpu_custom_call" | custom-call | tf_op jit(solution)/shard_map/vcycle/pallas_call | solution.py:514
  36.1 0.0 copy-start
  36.1 1.7 %copy.8 = f32[4,64,256]{2,1,0:T(8,128)} copy(f32[4,64,256]{2,1,0:T(8,128)} %get-tuple-element.4) | data formatting | bytes 524288
  37.8 0.0 copy-done
  37.8 0.7 %copy.9 = f32[4,64,256]{2,1,0:T(8,128)} copy(f32[4,64,256]{2,1,0:T(8,128)S(1)} %copy-done) | data formatting | bytes 524288
Async XLA Ops:
  36.1 1.7 %copy-start = (f32[4,64,256]{2,1,0:T(8,128)S(1)}, f32[4,64,256]{2,1,0:T(8,128)}, u32[]{:S(2)}) copy-start(f32[4,64,256]{2,1,0:T(8,128)} %get-tuple-element.5) | copy-start | bytes 786436

commit v3 on v2

--- a/solution.py
+++ b/solution.py
@@ -104,12 +104,12 @@
                 copy.wait_send()
 
 
-def kernel(n_alt, n_raan, f_hbm, ka_hbm, ki_hbm, kr_hbm, dens_hbm, sres_hbm,
-           ef, eka, eki, ekr, v1, v2, p0, p1, p2, wa, wi, wr, invd, diag, sres,
+def kernel(n_alt, n_raan, f_hbm, ka_hbm, ki_hbm, kr_hbm, dens, sres,
+           ef, eka, eki, ekr, v1, v2, p0, p1, p2, wa, wi, wr, invd, diag,
            pack, rb, xb, tmp, tmp2,
            k2a, k2b, w2, sb4, rb4, rhs2, c2a, c2b, q0, q1, q2, rf,
-           k3, w3, r3, c3, s3, l3,
-           load_sem, out_sem, send_sem, recv_sem, near):
+           k3, w3, r3, c3, sk, lk,
+           load_sem, send_sem, recv_sem, near):
     a = lax.axis_index("alt")
     r = lax.axis_index("raan")
     m_lo = jnp.where(a == 0, 0.0, 1.0).astype(jnp.float32)
@@ -197,9 +197,22 @@
         for side, here in ((d, has_up(d)), (-d, has_down(d))):
             @pl.when(jnp.logical_not(here))
             def _():
-                l3[:, FAR + side] = jnp.zeros((2, 8, WIDE), jnp.float32)
+                lk[FAR + side] = jnp.zeros((2, 8, WIDE), jnp.float32)
+                r3[FAR + side] = jnp.zeros((8, WIDE), jnp.float32)
+                c3[0, FAR + side] = jnp.zeros((8, WIDE), jnp.float32)
 
     pl.semaphore_wait(barrier, 2 + has_up(1).astype(jnp.int32) + has_down(1).astype(jnp.int32))
+
+    def hear(step):
+        @pl.when(has_down(1))
+        def _():
+            pl.semaphore_wait(near.at[step, 0], 1)
+
+        @pl.when(has_up(1))
+        def _():
+            pl.semaphore_wait(near.at[step, 1], 1)
+
+    greet(near.at[0, 0], near.at[0, 1])
 
     low2, high2, low1, high1 = slice(0, 2), slice(2, 4), slice(0, 1), slice(3, 4)
     below2, above2, below1, above1 = slice(0, 2), slice(6, 8), slice(1, 2), slice(6, 7)
@@ -224,8 +237,6 @@
         ring.append((remote(pack.at[i, :, 0], rb.at[i, :, 0], raan_dev(-1)),
                      remote(pack.at[i, :, 1], rb.at[i, :, 1], raan_dev(1))))
 
-    greet(near.at[0, 0], near.at[0, 1])
-
     def unpack(first, last, dst, layer):
         for g in range(4):
             both = jnp.where(quarter == g, first, last)
@@ -238,6 +249,9 @@
             copy.wait_recv()
         relay.append(exchange([(rb.at[i, high2 if i < 2 else high1], xb.at[0, x_slot[i]])],
                               [(rb.at[i, low2 if i < 2 else low1], xb.at[1, x_slot[i]])]))
+        if i == 1:
+            hear(0)
+            greet(near.at[1, 0], near.at[1, 1])
         for l in range(OWN):
             unpack(rb[i, l, 0], rb[i, l, 1], ext[i], HALO + l)
 
@@ -319,21 +333,22 @@
     k3[FAR, 0] = coarsen_mid(k2a[2] + k2a[3])
     k3[FAR, 1] = coarsen_mid(k2b[2, 0] + k2b[3, 0])
     k3[FAR, 2] = coarsen_mid(k2b[2, 1] + k2b[3, 1])
-    coarse = exchange([(k2a.at[2:4], k2a.at[0:2]), (k2b.at[3], k2b.at[1])],
-                      [(k2a.at[2:4], k2a.at[4:6]), (k2b.at[2], k2b.at[4])])
-
-    def hear(step):
-        @pl.when(has_down(1))
-        def _():
-            pl.semaphore_wait(near.at[step, 0], 1)
-
-        @pl.when(has_up(1))
-        def _():
-            pl.semaphore_wait(near.at[step, 1], 1)
-
-    for step in range(2):
-        hear(step)
-        greet(near.at[step + 1, 0], near.at[step + 1, 1])
+    coarse_alt = exchange([(k2a.at[3], k2a.at[1])], [(k2a.at[2], k2a.at[4])])
+    coarse = exchange([(k2a.at[2], k2a.at[0]), (k2b.at[3], k2b.at[1])],
+                      [(k2a.at[3], k2a.at[5]), (k2b.at[2], k2b.at[4])])
+    sk[0] = jnp.where(low3, k3[FAR, 0], k3[FAR, 1])
+    sk[1] = k3[FAR, 2]
+    far_k = []
+
+    def send_far_k(d):
+        part = slice(0, 2) if d < FAR else slice(0, 1)
+        far_k.append(exchange([(sk.at[part], lk.at[FAR - d, part])], [(sk.at[part], lk.at[FAR + d, part])], d))
+
+    send_far_k(1)
+    send_far_k(2)
+    hear(1)
+    greet(near.at[2, 0], near.at[2, 1])
+    send_far_k(3)
 
     bulk.wait_recv()
     for copy in relay:
@@ -344,14 +359,7 @@
     layers(1, 3, fine_weights, first_sweep)
     layers(5, 7, fine_weights, first_sweep)
 
-    hear(2)
-    s3[0] = jnp.where(low3, k3[FAR, 0], k3[FAR, 1])
-    far_k = []
-    for d in range(1, FAR + 1):
-        far_k.append(exchange([(s3.at[0], l3.at[0, FAR - d])], [(s3.at[0], l3.at[0, FAR + d])], d))
-
-    coarse.wait_recv()
-    for x in range(1, 5):
+    def weights_mid(x):
         m_down = {2: m_lo, 4: m_hi}.get(x, 1.0)
         m_up = {1: m_lo, 3: m_hi}.get(x, 1.0)
         w_down, w_up, w_inc, w_raan, dg = coarse_weights(
@@ -359,14 +367,22 @@
         for n, value in enumerate((w_down, w_up, w_inc, w_raan, dg, OMEGA / dg)):
             w2[x, n] = value
 
-    swept.wait_recv()
-    layers(1, 7, functools.partial(sweep_fine, v1, v2))
+    second_sweep = functools.partial(sweep_fine, v1, v2)
+    layers(2, 6, second_sweep)
 
     def residual_fine(l):
         return target_fine(v2, l) - diag[l] * v2[l]
 
+    for l in (3, 4):
+        p2[l] = residual_fine(l)
+    swept.wait_recv()
+    second_sweep(1)
+    second_sweep(6)
+    coarse_alt.wait_recv()
+    weights_mid(2)
+    weights_mid(3)
     for j in range(2):
-        rhs2[2 + j] = coarsen_fine(residual_fine(2 + 2 * j) + residual_fine(3 + 2 * j))
+        rhs2[2 + j] = coarsen_fine(p2[3 + j] + residual_fine(2 + 3 * j))
         c2a[2 + j] = rhs2[2 + j] * w2[2 + j, 5]
     sb4[0, 0] = rhs2[3]
     sb4[0, 1] = c2a[2]
@@ -375,12 +391,11 @@
     mid = exchange([(sb4.at[0], rb4.at[0])], [(sb4.at[1], rb4.at[1])])
     dens2 = exchange([(v2.at[4], v2.at[0])], [(v2.at[3], v2.at[7])])
 
-    for copy in far_k:
-        copy.wait_recv()
-    for x in range(2 * FAR + 1):
-        if x != FAR:
-            k3[x, 0] = first_of(l3[0, x])
-            k3[x, 1] = second_of(l3[0, x])
+    hear(2)
+    send_far_k(4)
+    coarse.wait_recv()
+    weights_mid(1)
+    weights_mid(4)
 
     def weights_far(x):
         at = a + x - FAR
@@ -391,7 +406,19 @@
         for n, value in enumerate((w_down, w_up, w_inc, w_raan, OMEGA / dg)):
             w3[x, n] = value
 
-    weights_far(FAR)
+    def take_far(x):
+        k3[x, 0] = first_of(lk[x, 0])
+        if x not in (0, 2 * FAR):
+            k3[x, 1] = second_of(lk[x, 0])
+            k3[x, 2] = lk[x, 1]
+
+    for copy in far_k[0:3]:
+        copy.wait_recv()
+    for x in range(1, 2 * FAR):
+        if x != FAR:
+            take_far(x)
+    for x in range(2, 2 * FAR - 1):
+        weights_far(x)
 
     mid.wait_recv()
     rhs2[1] = rb4[0, 0]
@@ -412,24 +439,22 @@
     residual = [target_mid(c2b, x) - w2[x, 4] * c2b[x] for x in (2, 3)]
     r3[FAR] = coarsen_mid(residual[0] + residual[1])
     c3[0, FAR] = r3[FAR] * w3[FAR, 4]
-    s3[1] = jnp.where(low3, r3[FAR], k3[FAR, 2])
-    s3[2] = c3[0, FAR]
     far = []
     for d in range(FAR, 0, -1):
-        part = s3.at[1 if d < FAR else 2]
-        far.append(exchange([(part, l3.at[1, FAR - d])], [(part, l3.at[1, FAR + d])], d))
+        part = r3 if d < FAR else c3.at[0]
+        far.append(exchange([(part.at[FAR], part.at[FAR - d])], [(part.at[FAR], part.at[FAR + d])], d))
     ends = exchange([(c2b.at[2], c2b.at[0])], [(c2b.at[3], c2b.at[5])])
 
+    far_k[3].wait_recv()
+    for x in (0, 2 * FAR):
+        take_far(x)
+    for x in (1, 2 * FAR - 1):
+        weights_far(x)
     for copy in far:
         copy.wait_recv()
     for x in range(1, 2 * FAR):
         if x != FAR:
-            r3[x] = first_of(l3[1, x])
-            k3[x, 2] = second_of(l3[1, x])
-            weights_far(x)
             c3[0, x] = r3[x] * w3[x, 4]
-    for x in (0, 2 * FAR):
-        c3[0, x] = l3[1, x]
     for n in range(3):
         for x in range(1 + n, 2 * FAR - n):
             v = c3[n, x]
@@ -462,63 +487,59 @@
     correct(3)
     last_sweep = functools.partial(sweep_fine, p0, p1)
     layers(3, 5, last_sweep)
-    inner = exchange([(p1.at[4], p1.at[0])], [(p1.at[3], p1.at[7])])
+    inner = exchange([(p1.at[4, :, cols], p1.at[0, :, cols])], [(p1.at[3, :, cols], p1.at[7, :, cols])])
     dens2.wait_recv()
     up2.wait_recv()
     correct(1)
     correct(4)
     layers(1, 3, last_sweep)
     layers(5, 7, last_sweep)
-    layers(2, 6, functools.partial(sweep_fine, p1, p2))
-    outs = [pltpu.make_async_copy(p2.at[own, :, cols], dens_hbm, out_sem.at[0])]
-    outs[0].start()
+    def final_sweep(l):
+        sweep_fine(p1, p2, l)
+        dens[l - HALO] = p2[l, :, cols]
 
     def last_residual(l):
         value = (1.0 / OMEGA) * (invd[l] * target_fine(p2, l)) - p2[l]
         sres[l - HALO] = value[:, 0:COLS]
 
+    layers(2, 6, final_sweep)
     layers(3, 5, last_residual)
     inner.wait_recv()
     sweep_fine(p1, p2, 1)
     sweep_fine(p1, p2, 6)
     last_residual(2)
     last_residual(5)
-    outs.append(pltpu.make_async_copy(sres, sres_hbm, out_sem.at[1]))
-    outs[1].start()
     for copy in sends:
         copy.wait_send()
-    for copy in outs:
-        copy.wait()
 
 
 def solution(mesh):
     n_alt, n_raan = mesh.shape["alt"], mesh.shape["raan"]
     spec = P("alt", None, "raan")
-    anywhere = pl.BlockSpec(memory_space=pl.ANY)
 
     def vmem(*shape):
         return pltpu.VMEM(shape, jnp.float32)
 
     def shards(source, k_alt, k_inc, k_raan):
-        scratch = [vmem(LAYERS, INC, WIDE)] * 14 + [vmem(OWN, INC, COLS)]
+        scratch = [vmem(LAYERS, INC, WIDE)] * 14
         scratch += [vmem(4, OWN, 2, 16, 128), vmem(4, OWN, 2, 16, 128), vmem(2, 6, 2, 16, 128),
                     vmem(TILES, INC, 128), vmem(TILES, 16, 128)]
         scratch += [vmem(6, 16, WIDE), vmem(6, 2, 16, WIDE), vmem(6, 6, 16, WIDE), vmem(2, 2, 16, WIDE),
                     vmem(2, 2, 16, WIDE)] + [vmem(6, 16, WIDE)] * 6 + [vmem(6, INC, WIDE)]
         scratch += [vmem(2 * FAR + 1, 3, 8, WIDE), vmem(2 * FAR + 1, 5, 8, WIDE), vmem(2 * FAR + 1, 8, WIDE),
-                    vmem(4, 2 * FAR + 1, 8, WIDE), vmem(3, 8, WIDE), vmem(2, 2 * FAR + 1, 8, WIDE)]
-        scratch += [pltpu.SemaphoreType.DMA((4,)), pltpu.SemaphoreType.DMA((2,)),
+                    vmem(4, 2 * FAR + 1, 8, WIDE), vmem(2, 8, WIDE), vmem(2 * FAR + 1, 2, 8, WIDE)]
+        scratch += [pltpu.SemaphoreType.DMA((4,)),
                     pltpu.SemaphoreType.DMA((64,)), pltpu.SemaphoreType.DMA((64,)),
                     pltpu.SemaphoreType.REGULAR((3, 2))]
-        shape = jax.ShapeDtypeStruct(source.shape, source.dtype)
+        shape = pltpu.VMEM(source.shape, source.dtype)
         return pl.pallas_call(
             functools.partial(kernel, n_alt, n_raan),
             out_shape=(shape, shape),
             in_specs=[pl.BlockSpec(memory_space=pltpu.HBM)] * 4,
-            out_specs=(anywhere, anywhere),
+            out_specs=(pl.BlockSpec(memory_space=pltpu.VMEM),) * 2,
             scratch_shapes=scratch,
             compiler_params=pltpu.CompilerParams(
-                collective_id=0, has_side_effects=True, vmem_limit_bytes=64 * 1024 * 1024 - 512 * 1024),
+                collective_id=0, has_side_effects=True, vmem_limit_bytes=60 * 1024 * 1024),
             name="vcycle",
         )(source, k_alt, k_inc, k_raan)
 

time: 38.6 us -> 34.3 us (0.89)
  Pallas kernels: 35.5 us -> 32.1 us
  local copies, waits for them, and re-layouts: 2.42 us -> 1.41 us
    pallas_call x1, Pallas kernels: 35.5 us -> 32.1 us  [shards(): pl.pallas_call(functools.partial(kernel, n_alt, n_raan), out_shape=(shape...]
    unnamed x4 -> x2, local copies, waits for them, and re-layouts: 2.42 us -> 1.41 us
where the time goes in v3:
time: 34.3 us; the launch traced here: 34.2 us
  Pallas kernels  32.1 us (94%)
  local copies, waits for them, and re-layouts  1.41 us (4%)
  between operations  0.64 us (2%)
    pallas_call x1, Pallas kernels, shards(): pl.pallas_call(functools.partial(kernel, n_alt, n_raan), out_shape=(shape...  32.1 us
    unnamed x2, local copies, waits for them, and re-layouts  1.41 us

profile of v3, /device:TPU:24, one launch (start us, length us, event | category | flops | bytes accessed | tf_op | source)
XLA Modules:
  0.0 34.2 jit_solution(5273054817803611778)
XLA Ops:
  0.6 32.1 %vcycle.1 = (f32[4,64,256]{2,1,0:T(8,128)S(1)}, f32[4,64,256]{2,1,0:T(8,128)S(1)}) custom-call(f32[4,64,256]{2,1,0:T(8,128)} %f_hbm.1, f32[4,64,256]{2,1,0:T(8,128)} %ka_hbm.1, f32[4,64,256]{2,1,0:T(8,128)} %ki_hbm.1, f32[4,64,256]{2,1,0:T(8,128)} %kr_hbm.1), custom_call_target="tpu_custom_call" | custom-call | tf_op jit(solution)/shard_map/vcycle/pallas_call | solution.py:535
  32.8 0.7 %copy.8 = f32[4,64,256]{2,1,0:T(8,128)} copy(f32[4,64,256]{2,1,0:T(8,128)S(1)} %get-tuple-element.2) | data formatting | bytes 524288
  33.5 0.7 %copy.9 = f32[4,64,256]{2,1,0:T(8,128)} copy(f32[4,64,256]{2,1,0:T(8,128)S(1)} %get-tuple-element.3) | data formatting | bytes 524288

commit v4 on v3

--- a/solution.py
+++ b/solution.py
@@ -40,12 +40,16 @@
 
 def prev_row(v):
     turned = row_roll(v, 1)
-    return jnp.where(iota(v.shape, 0) == 0, lane_roll(turned, 1), turned)
+    top = turned[0:8]
+    top = jnp.where(iota(top.shape, 0) == 0, lane_roll(top, 1), top)
+    return top if v.shape[0] == 8 else jnp.concatenate([top, turned[8:]], axis=0)
 
 
 def next_row(v):
     turned = row_roll(v, -1)
-    return jnp.where(iota(v.shape, 0) == v.shape[0] - 1, lane_roll(turned, -1), turned)
+    end = turned[-8:]
+    end = jnp.where(iota(end.shape, 0) == 7, lane_roll(end, -1), end)
+    return end if v.shape[0] == 8 else jnp.concatenate([turned[:-8], end], axis=0)
 
 
 def coarse_weights(k_alt, k_down, k_up, m_down, m_up, k_inc, k_raan, factor, step):
@@ -107,8 +111,8 @@
 def kernel(n_alt, n_raan, f_hbm, ka_hbm, ki_hbm, kr_hbm, dens, sres,
            ef, eka, eki, ekr, v1, v2, p0, p1, p2, wa, wi, wr, invd, diag,
            pack, rb, xb, tmp, tmp2,
-           k2a, k2b, w2, sb4, rb4, rhs2, c2a, c2b, q0, q1, q2, rf,
-           k3, w3, r3, c3, sk, lk,
+           k2a, k2b, w2, sb4, rb4, rhs2, c2a, c2b, q2, rf,
+           k3, w3, r3, sk, lk, sr, lr,
            load_sem, send_sem, recv_sem, near):
     a = lax.axis_index("alt")
     r = lax.axis_index("raan")
@@ -197,9 +201,8 @@
         for side, here in ((d, has_up(d)), (-d, has_down(d))):
             @pl.when(jnp.logical_not(here))
             def _():
-                lk[FAR + side] = jnp.zeros((2, 8, WIDE), jnp.float32)
-                r3[FAR + side] = jnp.zeros((8, WIDE), jnp.float32)
-                c3[0, FAR + side] = jnp.zeros((8, WIDE), jnp.float32)
+                lk[FAR + side] = jnp.zeros((3, 4, WIDE), jnp.float32)
+                lr[FAR + side] = jnp.zeros((4, WIDE), jnp.float32)
 
     pl.semaphore_wait(barrier, 2 + has_up(1).astype(jnp.int32) + has_down(1).astype(jnp.int32))
 
@@ -258,8 +261,8 @@
     row0 = iota((INC, WIDE), 0) == 0
 
     def fine_weights(l):
-        m_down = jnp.where(l == HALO, m_lo, jnp.where(l == HALO + OWN, m_hi, 1.0))
-        m_up = jnp.where(l == HALO - 1, m_lo, jnp.where(l == HALO + OWN - 1, m_hi, 1.0))
+        m_down = {HALO: m_lo, HALO + OWN: m_hi}.get(l, 1.0)
+        m_up = {HALO - 1: m_lo, HALO + OWN - 1: m_hi}.get(l, 1.0)
         k_alt = eka[l]
         lo = 0.5 * (k_alt + m_down * eka[l - 1])
         hi = 0.5 * (k_alt + m_up * eka[l + 1])
@@ -282,26 +285,57 @@
         dst[l] = 0.25 * src[l] + invd[l] * target_fine(src, l)
 
     def layers(lo, hi, *bodies):
-        def body(l, carry):
+        for l in range(lo, hi):
             for one in bodies:
                 one(l)
-            return carry
-        lax.fori_loop(lo, hi, body, 0)
 
     first_sweep = functools.partial(sweep_fine, ef, v1)
     layers(3, 5, fine_weights, first_sweep)
     swept = exchange([(v1.at[4], v1.at[0])], [(v1.at[3], v1.at[7])])
 
+    def edge_before(l, inner):
+        face = wa[min(l, inner)]
+        k_inc = eki[l]
+        w_inc = jnp.where(row0, 0.0, 0.5 * (k_inc + row_roll(k_inc, 1)))
+        k_raan = ekr[l]
+        w_raan = 0.5 * (k_raan + lane_roll(k_raan, 1))
+        wi[l] = w_inc
+        wr[l] = w_raan
+        diag[l] = 1.0 + (face + w_inc + row_roll(w_inc, -1) + w_raan + lane_roll(w_raan, -1))
+        v = ef[l]
+        total = v + face * ef[inner] + w_inc * row_roll(v, 1) + row_roll(w_inc * v, -1)
+        v1[l] = total + w_raan * lane_roll(v, 1) + lane_roll(w_raan * v, -1)
+
+    def edge_after(l, outer, m):
+        face = 0.5 * (eka[l] + m * eka[outer])
+        dg = diag[l] + face
+        inv = OMEGA / dg
+        wa[min(l, outer)] = m * face
+        diag[l] = dg
+        invd[l] = inv
+        v1[l] = 0.25 * ef[l] + inv * (v1[l] + (m * face) * ef[outer])
+
+    edge_before(2, 3)
+    edge_before(5, 4)
+
     even2 = iota((16, WIDE), 1) % 2 == 0
 
-    def row_pairs(scratch, x):
+    slot_of = [0]
+
+    def fresh(scratch):
+        slot_of[0] += 1
+        return scratch.at[slot_of[0] % scratch.shape[0]]
+
+    def row_pairs(slots, x):
+        scratch = fresh(slots)
         n = x.shape[0] // 2
         for t in range(TILES):
             scratch[t] = x[:, 128 * t:128 * t + 128]
         return jnp.concatenate(
             [scratch[t, pl.ds(0, n, stride=2)] + scratch[t, pl.ds(1, n, stride=2)] for t in range(TILES)], axis=1)
 
-    def twice(scratch, x):
+    def twice(slots, x):
+        scratch = fresh(slots)
         n = x.shape[0]
         for t in range(TILES):
             part = x[:, 128 * t:128 * t + 128]
@@ -320,11 +354,14 @@
         t = row_pairs(tmp2, total)
         return 0.125 * (t + jnp.where(low3, lane_roll(t, -2), lane_roll(t, 2)))
 
-    def first_of(pair):
-        return jnp.where(low3, pair, lane_roll(pair, 2))
-
-    def second_of(pair):
-        return jnp.where(low3, lane_roll(pair, -2), pair)
+    def fold(x):
+        return jnp.where(low3, x, row_roll(x, 4))[0:4]
+
+    upper3 = iota((8, WIDE), 0) < 4
+
+    def unfold(part):
+        both = jnp.concatenate([part, part], axis=0)
+        return jnp.where(upper3, jnp.where(low3, both, lane_roll(both, 2)), jnp.where(low3, lane_roll(both, -2), both))
 
     for j in range(2):
         k2a[2 + j] = coarsen_fine(eka[2 + 2 * j] + eka[3 + 2 * j])
@@ -336,28 +373,30 @@
     coarse_alt = exchange([(k2a.at[3], k2a.at[1])], [(k2a.at[2], k2a.at[4])])
     coarse = exchange([(k2a.at[2], k2a.at[0]), (k2b.at[3], k2b.at[1])],
                       [(k2a.at[3], k2a.at[5]), (k2b.at[2], k2b.at[4])])
-    sk[0] = jnp.where(low3, k3[FAR, 0], k3[FAR, 1])
-    sk[1] = k3[FAR, 2]
+    for n in range(3):
+        sk[n] = fold(k3[FAR, n])
     far_k = []
 
     def send_far_k(d):
-        part = slice(0, 2) if d < FAR else slice(0, 1)
+        part = slice(0, 3) if d < FAR else slice(0, 1)
         far_k.append(exchange([(sk.at[part], lk.at[FAR - d, part])], [(sk.at[part], lk.at[FAR + d, part])], d))
 
     send_far_k(1)
-    send_far_k(2)
     hear(1)
     greet(near.at[2, 0], near.at[2, 1])
-    send_far_k(3)
 
     bulk.wait_recv()
-    for copy in relay:
-        copy.wait_recv()
-    for side, two, one in ((0, (0, 1), 1), (1, (6, 7), 6)):
-        for i, slot, layer in ((0, 0, two[0]), (0, 1, two[1]), (1, 2, two[0]), (1, 3, two[1]), (2, 4, one), (3, 5, one)):
-            unpack(xb[side, slot, 0], xb[side, slot, 1], ext[i], layer)
-    layers(1, 3, fine_weights, first_sweep)
-    layers(5, 7, fine_weights, first_sweep)
+    for i, slots in ((0, (0, 1)), (1, (2, 3)), (2, (4,)), (3, (5,))):
+        relay[i].wait_recv()
+        for n, slot in enumerate(slots):
+            unpack(xb[0, slot, 0], xb[0, slot, 1], ext[i], n if len(slots) == 2 else 1)
+            unpack(xb[1, slot, 0], xb[1, slot, 1], ext[i], 6 + n)
+        if i == 1:
+            edge_after(2, 1, m_lo)
+            edge_after(5, 6, m_hi)
+    for l in (1, 6):
+        fine_weights(l)
+        first_sweep(l)
 
     def weights_mid(x):
         m_down = {2: m_lo, 4: m_hi}.get(x, 1.0)
@@ -389,8 +428,9 @@
     sb4[1, 0] = rhs2[2]
     sb4[1, 1] = c2a[3]
     mid = exchange([(sb4.at[0], rb4.at[0])], [(sb4.at[1], rb4.at[1])])
-    dens2 = exchange([(v2.at[4], v2.at[0])], [(v2.at[3], v2.at[7])])
-
+
+    send_far_k(2)
+    send_far_k(3)
     hear(2)
     send_far_k(4)
     coarse.wait_recv()
@@ -407,69 +447,70 @@
             w3[x, n] = value
 
     def take_far(x):
-        k3[x, 0] = first_of(lk[x, 0])
-        if x not in (0, 2 * FAR):
-            k3[x, 1] = second_of(lk[x, 0])
-            k3[x, 2] = lk[x, 1]
-
-    for copy in far_k[0:3]:
+        for n in range(1 if x in (0, 2 * FAR) else 3):
+            k3[x, n] = unfold(lk[x, n])
+
+    far_k[0].wait_recv()
+    take_far(FAR - 1)
+    take_far(FAR + 1)
+    weights_far(FAR)
+
+    mid.wait_recv()
+    rhs2[1] = rb4[0, 0]
+    rhs2[4] = rb4[1, 0]
+
+    def target_mid(values, x):
+        return rhs2[x] + beside_coarse(
+            values[x], values[x - 1], values[x + 1], w2[x, 0], w2[x, 1], w2[x, 2], w2[x, 3], 2)
+
+    def sweep_mid(values, x):
+        return 0.25 * values[x] + w2[x, 5] * target_mid(values, x)
+
+    before = [rb4[0, 1], rb4[0, 0] * w2[1, 5], c2a[2], c2a[3], rb4[1, 0] * w2[4, 5], rb4[1, 1]]
+    before[1:5] = [sweep_mid(before, x) for x in range(1, 5)]
+    residual = [target_mid(before, x) - w2[x, 4] * before[x] for x in (2, 3)]
+    r3[FAR] = coarsen_mid(residual[0] + residual[1])
+    sr[0] = fold(r3[FAR])
+    first3 = r3[FAR] * w3[FAR, 4]
+    sr[1] = fold(first3)
+    far = []
+    for d in range(FAR, 0, -1):
+        part = sr.at[0 if d < FAR else 1]
+        far.append(exchange([(part, lr.at[FAR - d])], [(part, lr.at[FAR + d])], d))
+    for x in range(1, 5):
+        c2b[x] = before[x]
+    ends = exchange([(c2b.at[2], c2b.at[0])], [(c2b.at[3], c2b.at[5])])
+    dens2 = exchange([(v2.at[4], v2.at[0])], [(v2.at[3], v2.at[7])])
+
+    for copy in far_k[1:]:
         copy.wait_recv()
+    for x in range(2 * FAR + 1):
+        if abs(x - FAR) > 1:
+            take_far(x)
     for x in range(1, 2 * FAR):
         if x != FAR:
-            take_far(x)
-    for x in range(2, 2 * FAR - 1):
-        weights_far(x)
-
-    mid.wait_recv()
-    rhs2[1] = rb4[0, 0]
-    c2a[0] = rb4[0, 1]
-    rhs2[4] = rb4[1, 0]
-    c2a[5] = rb4[1, 1]
-    c2a[1] = rhs2[1] * w2[1, 5]
-    c2a[4] = rhs2[4] * w2[4, 5]
-
-    def target_mid(src, x):
-        return rhs2[x] + beside_coarse(src[x], src[x - 1], src[x + 1], w2[x, 0], w2[x, 1], w2[x, 2], w2[x, 3], 2)
-
-    def sweep_mid(src, dst, x):
-        dst[x] = 0.25 * src[x] + w2[x, 5] * target_mid(src, x)
-
-    for x in range(1, 5):
-        sweep_mid(c2a, c2b, x)
-    residual = [target_mid(c2b, x) - w2[x, 4] * c2b[x] for x in (2, 3)]
-    r3[FAR] = coarsen_mid(residual[0] + residual[1])
-    c3[0, FAR] = r3[FAR] * w3[FAR, 4]
-    far = []
-    for d in range(FAR, 0, -1):
-        part = r3 if d < FAR else c3.at[0]
-        far.append(exchange([(part.at[FAR], part.at[FAR - d])], [(part.at[FAR], part.at[FAR + d])], d))
-    ends = exchange([(c2b.at[2], c2b.at[0])], [(c2b.at[3], c2b.at[5])])
-
-    far_k[3].wait_recv()
-    for x in (0, 2 * FAR):
-        take_far(x)
-    for x in (1, 2 * FAR - 1):
-        weights_far(x)
+            weights_far(x)
     for copy in far:
         copy.wait_recv()
-    for x in range(1, 2 * FAR):
+    for x in range(2 * FAR + 1):
         if x != FAR:
-            c3[0, x] = r3[x] * w3[x, 4]
+            r3[x] = unfold(lr[x])
+    v3 = [r3[x] if x in (0, 2 * FAR) else r3[x] * w3[x, 4] for x in range(2 * FAR + 1)]
     for n in range(3):
+        old = list(v3)
         for x in range(1 + n, 2 * FAR - n):
-            v = c3[n, x]
-            total = r3[x] + beside_coarse(v, c3[n, x - 1], c3[n, x + 1], w3[x, 0], w3[x, 1], w3[x, 2], w3[x, 3], 4)
-            c3[n + 1, x] = 0.25 * v + w3[x, 4] * total
+            total = r3[x] + beside_coarse(old[x], old[x - 1], old[x + 1], w3[x, 0], w3[x, 1], w3[x, 2], w3[x, 3], 4)
+            v3[x] = 0.25 * old[x] + w3[x, 4] * total
 
     ends.wait_recv()
+    after = [None] * 6
     for j in range(3):
-        part = twice(tmp2, c3[3, FAR - 1 + j])
+        part = twice(tmp2, v3[FAR - 1 + j])
         for x in (2 * j, 2 * j + 1):
-            q0[x] = c2b[x] + part
-    for x in range(1, 5):
-        sweep_mid(q0, q1, x)
+            after[x] = c2b[x] + part
+    after[1:5] = [sweep_mid(after, x) for x in range(1, 5)]
     for x in (2, 3):
-        sweep_mid(q1, q2, x)
+        q2[x] = sweep_mid(after, x)
     up2 = exchange([(q2.at[3], q2.at[1])], [(q2.at[2], q2.at[4])])
 
     def refine_mid(x):
@@ -523,11 +564,12 @@
     def shards(source, k_alt, k_inc, k_raan):
         scratch = [vmem(LAYERS, INC, WIDE)] * 14
         scratch += [vmem(4, OWN, 2, 16, 128), vmem(4, OWN, 2, 16, 128), vmem(2, 6, 2, 16, 128),
-                    vmem(TILES, INC, 128), vmem(TILES, 16, 128)]
+                    vmem(4, TILES, INC, 128), vmem(4, TILES, 16, 128)]
         scratch += [vmem(6, 16, WIDE), vmem(6, 2, 16, WIDE), vmem(6, 6, 16, WIDE), vmem(2, 2, 16, WIDE),
-                    vmem(2, 2, 16, WIDE)] + [vmem(6, 16, WIDE)] * 6 + [vmem(6, INC, WIDE)]
+                    vmem(2, 2, 16, WIDE)] + [vmem(6, 16, WIDE)] * 4 + [vmem(6, INC, WIDE)]
         scratch += [vmem(2 * FAR + 1, 3, 8, WIDE), vmem(2 * FAR + 1, 5, 8, WIDE), vmem(2 * FAR + 1, 8, WIDE),
-                    vmem(4, 2 * FAR + 1, 8, WIDE), vmem(2, 8, WIDE), vmem(2 * FAR + 1, 2, 8, WIDE)]
+                    vmem(3, 4, WIDE), vmem(2 * FAR + 1, 3, 4, WIDE),
+                    vmem(2, 4, WIDE), vmem(2 * FAR + 1, 4, WIDE)]
         scratch += [pltpu.SemaphoreType.DMA((4,)),
                     pltpu.SemaphoreType.DMA((64,)), pltpu.SemaphoreType.DMA((64,)),
                     pltpu.SemaphoreType.REGULAR((3, 2))]

time: 34.3 us -> 33.5 us (0.977)
  Pallas kernels: 32.1 us -> 31.3 us
    pallas_call x1, Pallas kernels: 32.1 us -> 31.3 us  [shards(): pl.pallas_call(functools.partial(kernel, n_alt, n_raan), out_shape=(shape...]
where the time goes in v4:
time: 33.5 us; the launch traced here: 33.4 us
  Pallas kernels  31.3 us (93%)
  local copies, waits for them, and re-layouts  1.41 us (4%)
  between operations  0.64 us (2%)
    pallas_call x1, Pallas kernels, shards(): pl.pallas_call(functools.partial(kernel, n_alt, n_raan), out_shape=(shape...  31.3 us
    unnamed x2, local copies, waits for them, and re-layouts  1.41 us

profile of v4, /device:TPU:24, one launch (start us, length us, event | category | flops | bytes accessed | tf_op | source)
XLA Modules:
  0.0 33.4 jit_solution(10254712853479295603)
XLA Ops:
  0.6 31.3 %vcycle.1 = (f32[4,64,256]{2,1,0:T(8,128)S(1)}, f32[4,64,256]{2,1,0:T(8,128)S(1)}) custom-call(f32[4,64,256]{2,1,0:T(8,128)} %f_hbm.1, f32[4,64,256]{2,1,0:T(8,128)} %ka_hbm.1, f32[4,64,256]{2,1,0:T(8,128)} %ki_hbm.1, f32[4,64,256]{2,1,0:T(8,128)} %kr_hbm.1), custom_call_target="tpu_custom_call" | custom-call | tf_op jit(solution)/shard_map/vcycle/pallas_call | solution.py:577
  32.0 0.7 %copy.8 = f32[4,64,256]{2,1,0:T(8,128)} copy(f32[4,64,256]{2,1,0:T(8,128)S(1)} %get-tuple-element.2) | data formatting | bytes 524288
  32.7 0.7 %copy.9 = f32[4,64,256]{2,1,0:T(8,128)} copy(f32[4,64,256]{2,1,0:T(8,128)S(1)} %get-tuple-element.3) | data formatting | bytes 524288

commit v5 on v4

--- a/solution.py
+++ b/solution.py
@@ -108,7 +108,7 @@
                 copy.wait_send()
 
 
-def kernel(n_alt, n_raan, f_hbm, ka_hbm, ki_hbm, kr_hbm, dens, sres,
+def kernel(n_alt, n_raan, f_hbm, ka_hbm, ki_hbm, kr_hbm, result,
            ef, eka, eki, ekr, v1, v2, p0, p1, p2, wa, wi, wr, invd, diag,
            pack, rb, xb, tmp, tmp2,
            k2a, k2b, w2, sb4, rb4, rhs2, c2a, c2b, q2, rf,
@@ -204,27 +204,7 @@
                 lk[FAR + side] = jnp.zeros((3, 4, WIDE), jnp.float32)
                 lr[FAR + side] = jnp.zeros((4, WIDE), jnp.float32)
 
-    pl.semaphore_wait(barrier, 2 + has_up(1).astype(jnp.int32) + has_down(1).astype(jnp.int32))
-
-    def hear(step):
-        @pl.when(has_down(1))
-        def _():
-            pl.semaphore_wait(near.at[step, 0], 1)
-
-        @pl.when(has_up(1))
-        def _():
-            pl.semaphore_wait(near.at[step, 1], 1)
-
-    greet(near.at[0, 0], near.at[0, 1])
-
-    low2, high2, low1, high1 = slice(0, 2), slice(2, 4), slice(0, 1), slice(3, 4)
-    below2, above2, below1, above1 = slice(0, 2), slice(6, 8), slice(1, 2), slice(6, 7)
-    bulk = exchange(
-        [(hbm[i].at[high2 if i < 2 else high1], ext[i].at[below2 if i < 2 else below1, :, cols]) for i in range(4)],
-        [(hbm[i].at[low2 if i < 2 else low1], ext[i].at[above2 if i < 2 else above1, :, cols]) for i in range(4)])
-
     quarter = iota((16, 128), 1) // 32
-    ring = []
     for i in range(4):
         loads[i].wait()
         for l in range(OWN):
@@ -237,8 +217,30 @@
                 last = jnp.where(quarter == (3 + g) % 4, lane_roll(high[16 * g:16 * g + 16], 32 * g), last)
             pack[i, l, 0] = first
             pack[i, l, 1] = last
+
+    pl.semaphore_wait(barrier, 2 + has_up(1).astype(jnp.int32) + has_down(1).astype(jnp.int32))
+
+    def hear(step):
+        @pl.when(has_down(1))
+        def _():
+            pl.semaphore_wait(near.at[step, 0], 1)
+
+        @pl.when(has_up(1))
+        def _():
+            pl.semaphore_wait(near.at[step, 1], 1)
+
+    greet(near.at[0, 0], near.at[0, 1])
+
+    ring = []
+    for i in range(4):
         ring.append((remote(pack.at[i, :, 0], rb.at[i, :, 0], raan_dev(-1)),
                      remote(pack.at[i, :, 1], rb.at[i, :, 1], raan_dev(1))))
+
+    low2, high2, low1, high1 = slice(0, 2), slice(2, 4), slice(0, 1), slice(3, 4)
+    below2, above2, below1, above1 = slice(0, 2), slice(6, 8), slice(1, 2), slice(6, 7)
+    bulk = exchange(
+        [(hbm[i].at[high2 if i < 2 else high1], ext[i].at[below2 if i < 2 else below1, :, cols]) for i in range(4)],
+        [(hbm[i].at[low2 if i < 2 else low1], ext[i].at[above2 if i < 2 else above1, :, cols]) for i in range(4)])
 
     def unpack(first, last, dst, layer):
         for g in range(4):
@@ -255,7 +257,7 @@
         if i == 1:
             hear(0)
             greet(near.at[1, 0], near.at[1, 1])
-        for l in range(OWN):
+        for l in range(OWN) if i < 2 else (1, 2):
             unpack(rb[i, l, 0], rb[i, l, 1], ext[i], HALO + l)
 
     row0 = iota((INC, WIDE), 0) == 0
@@ -315,6 +317,9 @@
         invd[l] = inv
         v1[l] = 0.25 * ef[l] + inv * (v1[l] + (m * face) * ef[outer])
 
+    for i in (2, 3):
+        for l in (0, 3):
+            unpack(rb[i, l, 0], rb[i, l, 1], ext[i], HALO + l)
     edge_before(2, 3)
     edge_before(5, 4)
 
@@ -537,11 +542,11 @@
     layers(5, 7, last_sweep)
     def final_sweep(l):
         sweep_fine(p1, p2, l)
-        dens[l - HALO] = p2[l, :, cols]
+        result[l - HALO] = p2[l, :, cols]
 
     def last_residual(l):
         value = (1.0 / OMEGA) * (invd[l] * target_fine(p2, l)) - p2[l]
-        sres[l - HALO] = value[:, 0:COLS]
+        result[l - HALO + OWN] = value[:, 0:COLS]
 
     layers(2, 6, final_sweep)
     layers(3, 5, last_residual)
@@ -573,16 +578,17 @@
         scratch += [pltpu.SemaphoreType.DMA((4,)),
                     pltpu.SemaphoreType.DMA((64,)), pltpu.SemaphoreType.DMA((64,)),
                     pltpu.SemaphoreType.REGULAR((3, 2))]
-        shape = pltpu.VMEM(source.shape, source.dtype)
-        return pl.pallas_call(
+        shape = pltpu.VMEM((2 * OWN, INC, COLS), source.dtype)
+        result = pl.pallas_call(
             functools.partial(kernel, n_alt, n_raan),
-            out_shape=(shape, shape),
+            out_shape=shape,
             in_specs=[pl.BlockSpec(memory_space=pltpu.HBM)] * 4,
-            out_specs=(pl.BlockSpec(memory_space=pltpu.VMEM),) * 2,
+            out_specs=pl.BlockSpec(memory_space=pltpu.VMEM),
             scratch_shapes=scratch,
             compiler_params=pltpu.CompilerParams(
                 collective_id=0, has_side_effects=True, vmem_limit_bytes=60 * 1024 * 1024),
             name="vcycle",
         )(source, k_alt, k_inc, k_raan)
+        return result[:OWN], result[OWN:]
 
     return jax.shard_map(shards, mesh=mesh, in_specs=(spec,) * 4, out_specs=(spec, spec), check_vma=False)

time: 33.5 us -> 32.8 us (0.979)
  local copies, waits for them, and re-layouts: 1.41 us -> 0.83 us
  Pallas kernels: 31.3 us -> 30.9 us
    unnamed x2 -> x0, local copies, waits for them, and re-layouts: 1.41 us -> none
    slice x0 -> x1, local copies, waits for them, and re-layouts: none -> 0.83 us  [shards(): return (result[:OWN], result[OWN:])]
    pallas_call x1, Pallas kernels: 31.3 us -> 30.9 us  [shards(): pl.pallas_call(functools.partial(kernel, n_alt, n_raan), out_shape=shape,...]
where the time goes in v5:
time: 32.8 us; the launch traced here: 32.4 us
  Pallas kernels  30.9 us (94%)
  local copies, waits for them, and re-layouts  0.83 us (3%)
  between operations  0.64 us (2%)
    pallas_call x1, Pallas kernels, shards(): pl.pallas_call(functools.partial(kernel, n_alt, n_raan), out_shape=shape,...  30.9 us
    slice x1, local copies, waits for them, and re-layouts, shards(): return (result[:OWN], result[OWN:])  0.83 us

profile of v5, /device:TPU:24, one launch (start us, length us, event | category | flops | bytes accessed | tf_op | source)
XLA Modules:
  0.0 32.4 jit_solution(8138275454711088413)
XLA Ops:
  0.6 30.9 %vcycle.1 = f32[8,64,256]{2,1,0:T(8,128)S(1)} custom-call(f32[4,64,256]{2,1,0:T(8,128)} %f_hbm.1, f32[4,64,256]{2,1,0:T(8,128)} %ka_hbm.1, f32[4,64,256]{2,1,0:T(8,128)} %ki_hbm.1, f32[4,64,256]{2,1,0:T(8,128)} %kr_hbm.1), custom_call_target="tpu_custom_call" | custom-call | tf_op jit(solution)/shard_map/vcycle/pallas_call | solution.py:582
  31.6 0.8 %fusion = (f32[4,64,256]{2,1,0:T(8,128)}, f32[4,64,256]{2,1,0:T(8,128)}) fusion(f32[8,64,256]{2,1,0:T(8,128)S(1)} %vcycle.1), kind=kLoop, calls=%fused_computation | loop fusion | bytes 1048576 | tf_op jit(solution)/shard_map/slice | solution.py:592

commit v6 on v5

--- a/solution.py
+++ b/solution.py
@@ -110,7 +110,7 @@
 
 def kernel(n_alt, n_raan, f_hbm, ka_hbm, ki_hbm, kr_hbm, result,
            ef, eka, eki, ekr, v1, v2, p0, p1, p2, wa, wi, wr, invd, diag,
-           pack, rb, xb, tmp, tmp2,
+           pack, rb, xb, vs, vr, tmp, tmp2,
            k2a, k2b, w2, sb4, rb4, rhs2, c2a, c2b, q2, rf,
            k3, w3, r3, sk, lk, sr, lr,
            load_sem, send_sem, recv_sem, near):
@@ -184,6 +184,7 @@
         for ref in (ef, eka, eki, ekr, v1, v2, p1):
             ref[0:HALO] = jnp.zeros((HALO, INC, WIDE), jnp.float32)
         xb[0] = jnp.zeros(xb.shape[1:], jnp.float32)
+        vr[0] = jnp.zeros(vr.shape[1:], jnp.float32)
         rb4[0] = jnp.zeros(rb4.shape[1:], jnp.float32)
         for ref in (k2a, k2b, c2b, q2):
             ref[0:2] = jnp.zeros((2,) + ref.shape[1:], jnp.float32)
@@ -193,6 +194,7 @@
         for ref in (ef, eka, eki, ekr, v1, v2, p1):
             ref[HALO + OWN:LAYERS] = jnp.zeros((HALO, INC, WIDE), jnp.float32)
         xb[1] = jnp.zeros(xb.shape[1:], jnp.float32)
+        vr[1] = jnp.zeros(vr.shape[1:], jnp.float32)
         rb4[1] = jnp.zeros(rb4.shape[1:], jnp.float32)
         for ref in (k2a, k2b, c2b, q2):
             ref[4:6] = jnp.zeros((2,) + ref.shape[1:], jnp.float32)
@@ -239,8 +241,10 @@
     low2, high2, low1, high1 = slice(0, 2), slice(2, 4), slice(0, 1), slice(3, 4)
     below2, above2, below1, above1 = slice(0, 2), slice(6, 8), slice(1, 2), slice(6, 7)
     bulk = exchange(
-        [(hbm[i].at[high2 if i < 2 else high1], ext[i].at[below2 if i < 2 else below1, :, cols]) for i in range(4)],
-        [(hbm[i].at[low2 if i < 2 else low1], ext[i].at[above2 if i < 2 else above1, :, cols]) for i in range(4)])
+        [(ext[i].at[slice(4, 6) if i < 2 else slice(5, 6), :, cols], ext[i].at[below2 if i < 2 else below1, :, cols])
+         for i in range(4)],
+        [(ext[i].at[slice(2, 4) if i < 2 else slice(2, 3), :, cols], ext[i].at[above2 if i < 2 else above1, :, cols])
+         for i in range(4)])
 
     def unpack(first, last, dst, layer):
         for g in range(4):
@@ -293,7 +297,12 @@
 
     first_sweep = functools.partial(sweep_fine, ef, v1)
     layers(3, 5, fine_weights, first_sweep)
-    swept = exchange([(v1.at[4], v1.at[0])], [(v1.at[3], v1.at[7])])
+    between = (iota((32, 128), 1) >= 32) & (iota((32, 128), 1) < 96)
+    for n, l in enumerate((4, 3)):
+        side = v1[l, :, COLS:WIDE]
+        vs[n] = jnp.where(between, lane_roll(side[32:64], 64), side[0:32])
+    swept = exchange([(v1.at[4, :, cols], v1.at[0, :, cols]), (vs.at[0], vr.at[0])],
+                     [(v1.at[3, :, cols], v1.at[7, :, cols]), (vs.at[1], vr.at[1])])
 
     def edge_before(l, inner):
         face = wa[min(l, inner)]
@@ -420,6 +429,9 @@
     for l in (3, 4):
         p2[l] = residual_fine(l)
     swept.wait_recv()
+    for n, l in enumerate((0, 7)):
+        v1[l, 0:32, COLS:WIDE] = vr[n]
+        v1[l, 32:64, COLS:WIDE] = lane_roll(vr[n], 64)
     second_sweep(1)
     second_sweep(6)
     coarse_alt.wait_recv()
@@ -534,12 +546,25 @@
     last_sweep = functools.partial(sweep_fine, p0, p1)
     layers(3, 5, last_sweep)
     inner = exchange([(p1.at[4, :, cols], p1.at[0, :, cols])], [(p1.at[3, :, cols], p1.at[7, :, cols])])
+
+    def last_before(l, inward):
+        v = p0[l]
+        total = ef[l] + wa[min(l, inward)] * p0[inward] + wi[l] * row_roll(v, 1) + row_roll(wi[l] * v, -1)
+        p1[l] = total + wr[l] * lane_roll(v, 1) + lane_roll(wr[l] * v, -1)
+
+    def last_after(l, outward):
+        p1[l] = 0.25 * p0[l] + invd[l] * (p1[l] + wa[min(l, outward)] * p0[outward])
+
+    last_before(2, 3)
+    last_before(5, 4)
     dens2.wait_recv()
     up2.wait_recv()
     correct(1)
     correct(4)
-    layers(1, 3, last_sweep)
-    layers(5, 7, last_sweep)
+    last_after(2, 1)
+    last_after(5, 6)
+    last_sweep(1)
+    last_sweep(6)
     def final_sweep(l):
         sweep_fine(p1, p2, l)
         result[l - HALO] = p2[l, :, cols]
@@ -568,7 +593,7 @@
 
     def shards(source, k_alt, k_inc, k_raan):
         scratch = [vmem(LAYERS, INC, WIDE)] * 14
-        scratch += [vmem(4, OWN, 2, 16, 128), vmem(4, OWN, 2, 16, 128), vmem(2, 6, 2, 16, 128),
+        scratch += [vmem(4, OWN, 2, 16, 128), vmem(4, OWN, 2, 16, 128), vmem(2, 6, 2, 16, 128), vmem(2, 32, 128), vmem(2, 32, 128),
                     vmem(4, TILES, INC, 128), vmem(4, TILES, 16, 128)]
         scratch += [vmem(6, 16, WIDE), vmem(6, 2, 16, WIDE), vmem(6, 6, 16, WIDE), vmem(2, 2, 16, WIDE),
                     vmem(2, 2, 16, WIDE)] + [vmem(6, 16, WIDE)] * 4 + [vmem(6, INC, WIDE)]

time: 32.8 us -> 32.3 us (0.985)
    pallas_call x1, Pallas kernels: 30.9 us -> 30.6 us  [shards(): pl.pallas_call(functools.partial(kernel, n_alt, n_raan), out_shape=shape,...]
where the time goes in v6:
time: 32.3 us; the launch traced here: 32.1 us
  Pallas kernels  30.6 us (95%)
  local copies, waits for them, and re-layouts  0.83 us (3%)
  between operations  0.64 us (2%)
    pallas_call x1, Pallas kernels, shards(): pl.pallas_call(functools.partial(kernel, n_alt, n_raan), out_shape=shape,...  30.6 us
    slice x1, local copies, waits for them, and re-layouts, shards(): return (result[:OWN], result[OWN:])  0.83 us

profile of v6, /device:TPU:24, one launch (start us, length us, event | category | flops | bytes accessed | tf_op | source)
XLA Modules:
  0.0 32.1 jit_solution(3532205852357002431)
XLA Ops:
  0.6 30.6 %vcycle.1 = f32[8,64,256]{2,1,0:T(8,128)S(1)} custom-call(f32[4,64,256]{2,1,0:T(8,128)} %f_hbm.1, f32[4,64,256]{2,1,0:T(8,128)} %ka_hbm.1, f32[4,64,256]{2,1,0:T(8,128)} %ki_hbm.1, f32[4,64,256]{2,1,0:T(8,128)} %kr_hbm.1), custom_call_target="tpu_custom_call" | custom-call | tf_op jit(solution)/shard_map/vcycle/pallas_call | solution.py:607
  31.2 0.8 %fusion = (f32[4,64,256]{2,1,0:T(8,128)}, f32[4,64,256]{2,1,0:T(8,128)}) fusion(f32[8,64,256]{2,1,0:T(8,128)S(1)} %vcycle.1), kind=kLoop, calls=%fused_computation | loop fusion | bytes 1048576 | tf_op jit(solution)/shard_map/slice | solution.py:617

commit v7 on v6

--- a/solution.py
+++ b/solution.py
@@ -344,7 +344,7 @@
         scratch = fresh(slots)
         n = x.shape[0] // 2
         for t in range(TILES):
-            scratch[t] = x[:, 128 * t:128 * t + 128]
+            scratch[t, 0:2 * n] = x[:, 128 * t:128 * t + 128]
         return jnp.concatenate(
             [scratch[t, pl.ds(0, n, stride=2)] + scratch[t, pl.ds(1, n, stride=2)] for t in range(TILES)], axis=1)
 
@@ -355,7 +355,7 @@
             part = x[:, 128 * t:128 * t + 128]
             scratch[t, pl.ds(0, n, stride=2)] = part
             scratch[t, pl.ds(1, n, stride=2)] = part
-        return jnp.concatenate([scratch[t] for t in range(TILES)], axis=1)
+        return jnp.concatenate([scratch[t, 0:2 * n] for t in range(TILES)], axis=1)
 
     def coarsen_fine(total):
         pairs = row_pairs(tmp, total)
@@ -594,12 +594,12 @@
     def shards(source, k_alt, k_inc, k_raan):
         scratch = [vmem(LAYERS, INC, WIDE)] * 14
         scratch += [vmem(4, OWN, 2, 16, 128), vmem(4, OWN, 2, 16, 128), vmem(2, 6, 2, 16, 128), vmem(2, 32, 128), vmem(2, 32, 128),
-                    vmem(4, TILES, INC, 128), vmem(4, TILES, 16, 128)]
+                    vmem(4, TILES, INC + 8, 128), vmem(4, TILES, 24, 128)]
         scratch += [vmem(6, 16, WIDE), vmem(6, 2, 16, WIDE), vmem(6, 6, 16, WIDE), vmem(2, 2, 16, WIDE),
                     vmem(2, 2, 16, WIDE)] + [vmem(6, 16, WIDE)] * 4 + [vmem(6, INC, WIDE)]
         scratch += [vmem(2 * FAR + 1, 3, 8, WIDE), vmem(2 * FAR + 1, 5, 8, WIDE), vmem(2 * FAR + 1, 8, WIDE),
-                    vmem(3, 4, WIDE), vmem(2 * FAR + 1, 3, 4, WIDE),
-                    vmem(2, 4, WIDE), vmem(2 * FAR + 1, 4, WIDE)]
+                    vmem(4, 4, WIDE), vmem(2 * FAR + 2, 3, 4, WIDE),
+                    vmem(3, 4, WIDE), vmem(2 * FAR + 2, 4, WIDE)]
         scratch += [pltpu.SemaphoreType.DMA((4,)),
                     pltpu.SemaphoreType.DMA((64,)), pltpu.SemaphoreType.DMA((64,)),
                     pltpu.SemaphoreType.REGULAR((3, 2))]

time: 32.3 us -> 32.3 us (level)
  no operation moved by 1% of the time
where the time goes in v7:
time: 32.3 us; the launch traced here: 32.1 us
  Pallas kernels  30.6 us (95%)
  local copies, waits for them, and re-layouts  0.83 us (3%)
  between operations  0.64 us (2%)
    pallas_call x1, Pallas kernels, shards(): pl.pallas_call(functools.partial(kernel, n_alt, n_raan), out_shape=shape,...  30.6 us
    slice x1, local copies, waits for them, and re-layouts, shards(): return (result[:OWN], result[OWN:])  0.83 us

profile of v7, /device:TPU:24, one launch (start us, length us, event | category | flops | bytes accessed | tf_op | source)
XLA Modules:
  0.0 32.1 jit_solution(17380097832552168130)
XLA Ops:
  0.6 30.6 %vcycle.1 = f32[8,64,256]{2,1,0:T(8,128)S(1)} custom-call(f32[4,64,256]{2,1,0:T(8,128)} %f_hbm.1, f32[4,64,256]{2,1,0:T(8,128)} %ka_hbm.1, f32[4,64,256]{2,1,0:T(8,128)} %ki_hbm.1, f32[4,64,256]{2,1,0:T(8,128)} %kr_hbm.1), custom_call_target="tpu_custom_call" | custom-call | tf_op jit(solution)/shard_map/vcycle/pallas_call | solution.py:607
  31.3 0.8 %fusion = (f32[4,64,256]{2,1,0:T(8,128)}, f32[4,64,256]{2,1,0:T(8,128)}) fusion(f32[8,64,256]{2,1,0:T(8,128)S(1)} %vcycle.1), kind=kLoop, calls=%fused_computation | loop fusion | bytes 1048576 | tf_op jit(solution)/shard_map/slice | solution.py:617

commit v8 on v7

--- a/solution.py
+++ b/solution.py
@@ -231,13 +231,6 @@
         def _():
             pl.semaphore_wait(near.at[step, 1], 1)
 
-    greet(near.at[0, 0], near.at[0, 1])
-
-    ring = []
-    for i in range(4):
-        ring.append((remote(pack.at[i, :, 0], rb.at[i, :, 0], raan_dev(-1)),
-                     remote(pack.at[i, :, 1], rb.at[i, :, 1], raan_dev(1))))
-
     low2, high2, low1, high1 = slice(0, 2), slice(2, 4), slice(0, 1), slice(3, 4)
     below2, above2, below1, above1 = slice(0, 2), slice(6, 8), slice(1, 2), slice(6, 7)
     bulk = exchange(
@@ -245,6 +238,13 @@
          for i in range(4)],
         [(ext[i].at[slice(2, 4) if i < 2 else slice(2, 3), :, cols], ext[i].at[above2 if i < 2 else above1, :, cols])
          for i in range(4)])
+
+    ring = []
+    for i in range(4):
+        ring.append((remote(pack.at[i, :, 0], rb.at[i, :, 0], raan_dev(-1)),
+                     remote(pack.at[i, :, 1], rb.at[i, :, 1], raan_dev(1))))
+
+    greet(near.at[0, 0], near.at[0, 1])
 
     def unpack(first, last, dst, layer):
         for g in range(4):

time: 32.3 us -> 32.2 us (level)
  no operation moved by 1% of the time
where the time goes in v8:
time: 32.2 us; the launch traced here: 32.1 us
  Pallas kernels  30.6 us (95%)
  local copies, waits for them, and re-layouts  0.83 us (3%)
  between operations  0.64 us (2%)
    pallas_call x1, Pallas kernels, shards(): pl.pallas_call(functools.partial(kernel, n_alt, n_raan), out_shape=shape,...  30.6 us
    slice x1, local copies, waits for them, and re-layouts, shards(): return (result[:OWN], result[OWN:])  0.83 us

profile of v8, /device:TPU:24, one launch (start us, length us, event | category | flops | bytes accessed | tf_op | source)
XLA Modules:
  0.0 32.1 jit_solution(17384442897809078013)
XLA Ops:
  0.6 30.6 %vcycle.1 = f32[8,64,256]{2,1,0:T(8,128)S(1)} custom-call(f32[4,64,256]{2,1,0:T(8,128)} %f_hbm.1, f32[4,64,256]{2,1,0:T(8,128)} %ka_hbm.1, f32[4,64,256]{2,1,0:T(8,128)} %ki_hbm.1, f32[4,64,256]{2,1,0:T(8,128)} %kr_hbm.1), custom_call_target="tpu_custom_call" | custom-call | tf_op jit(solution)/shard_map/vcycle/pallas_call | solution.py:607
  31.3 0.8 %fusion = (f32[4,64,256]{2,1,0:T(8,128)}, f32[4,64,256]{2,1,0:T(8,128)}) fusion(f32[8,64,256]{2,1,0:T(8,128)S(1)} %vcycle.1), kind=kLoop, calls=%fused_computation | loop fusion | bytes 1048576 | tf_op jit(solution)/shard_map/slice | solution.py:617
